TPU v7x, 32 devices: a whole 2x2x4 slice. The times are simulated.
32 devices in a mesh: dp: 2 (over x), ctx: 16 (over z, y, core).
Axes of the slice: x: 2, y: 2, z: 4, core: 2. Of those that a mesh axis runs over, the one named last changes fastest.
Arguments:
- queries: bfloat16 [4096, 2048], P(('dp', 'ctx')), parts along dimension 0, may hold values from -6 to 6
- key_rows: bfloat16 [4096, 2048], P(('dp', 'ctx')), parts along dimension 0, may hold values from -6 to 6
- value_rows: bfloat16 [4096, 2048], P(('dp', 'ctx')), parts along dimension 0, may hold values from -6 to 6
- attn_out: bfloat16 [4096, 2048], P(('dp', 'ctx')), parts along dimension 0, may hold values from -6 to 6
- out_grad: bfloat16 [4096, 2048], P(('dp', 'ctx')), parts along dimension 0, may hold values from -6 to 6
- log_norm: float32 [4096, 16], P(('dp', 'ctx')), parts along dimension 0, may hold values from 4 to 7
- segments: int32 [4096], P(('dp', 'ctx')), parts along dimension 0, may hold values from 0 to 7, never falling along the last dimension, each value on 1 to 896 neighbouring positions
Outputs:
- query_grad: bfloat16 [4096, 2048], P(('dp', 'ctx')), parts along dimension 0
- key_grad: bfloat16 [4096, 2048], P(('dp', 'ctx')), parts along dimension 0
- value_grad: bfloat16 [4096, 2048], P(('dp', 'ctx')), parts along dimension 0
There are 2 independent parts, one for each index of `dp`. A program takes and returns all parts, laid end to end along the dimension named above; each array names one. Nothing has to cross between parts.
Inputs may be any that keep to these rules, and one draw needn't show every extreme that they name: `segments`: never falls along the tokens; every document number is used; no document has more than 896 tokens and one has exactly 896.
All inputs are finite; a program needn't handle non-finite values.
Results may differ from a plain program's by a relative error of at most 0.0085.
Values may be sent and summed in bfloat16 or wider, within the bound.
A program may use at most 64 MiB of HBM per device.

v0:
```python
import jax
import jax.numpy as jnp
from jax import lax
from jax.sharding import PartitionSpec as P

HEAD_DIM = 128
SEQ_DEVS = 8


def shortened(value):

    def short(part):
        return part.astype(jnp.bfloat16) if part.dtype == jnp.float32 else part

    return jax.tree.map(short, value)


def from_behind(value, axis, by):
    size = lax.axis_size(axis)
    pairs = [(i, i + by) for i in range(size) if 0 <= i + by < size]
    return lax.ppermute(value, axis, pairs)


def passed_along(block, axis, distance):
    devices = range(lax.axis_size(axis))
    route = [((i - distance) % len(devices), i) for i in devices]
    return lax.ppermute(block, axis, route)


def head_view(matrix):
    return matrix.reshape(matrix.shape[0], -1, HEAD_DIM)


def live_pairs(query_pos, key_pos, query_seg, key_seg):
    same_doc = query_seg[:, None] == key_seg[None, :]
    causal = key_pos[None, :] <= query_pos[:, None]
    return same_doc & causal


def tile_terms(queries, out_grad, log_norm, row_delta, key_rows, value_rows, pattern):
    softmax_scale = HEAD_DIM ** (-0.5)
    scores = (
        jnp.einsum(
            "qhd,khd->hqk",
            head_view(queries),
            head_view(key_rows),
            preferred_element_type=jnp.float32,
        )
        * softmax_scale
    )
    attn_prob = jnp.where(pattern[None], jnp.exp(scores - log_norm.T[:, :, None]), 0.0)
    prob_grad = jnp.einsum(
        "qhd,khd->hqk",
        head_view(out_grad),
        head_view(value_rows),
        preferred_element_type=jnp.float32,
    )
    score_low = (attn_prob * (prob_grad - row_delta.T[:, :, None])).astype(jnp.bfloat16)
    results = []
    query_add = jnp.einsum(
        "hqk,khd->qhd", score_low, head_view(key_rows), preferred_element_type=jnp.float32
    )
    results.append(query_add.reshape(queries.shape[0], -1))
    key_add = jnp.einsum(
        "hqk,qhd->khd", score_low, head_view(queries), preferred_element_type=jnp.float32
    )
    value_add = jnp.einsum(
        "hqk,qhd->khd",
        attn_prob.astype(jnp.bfloat16),
        head_view(out_grad),
        preferred_element_type=jnp.float32,
    )
    results.append(key_add.reshape(key_rows.shape[0], -1))
    results.append(value_add.reshape(key_rows.shape[0], -1))
    return tuple(results)


def pass_queries(queries, out_grad, segments):
    return (
        from_behind(queries, "ctx", -1),
        from_behind(out_grad, "ctx", -1),
        from_behind(shortened(segments), "ctx", -1).astype(segments.dtype),
    )


def on_device(queries, key_rows, value_rows, attn_out, out_grad, log_norm, segments):
    tok_rows = queries.shape[0]
    chain_len = lax.axis_size("ctx")
    block_index = lax.axis_index("ctx")
    local_iota = lax.iota(jnp.int32, tok_rows)
    own_pos = block_index * tok_rows + local_iota
    row_delta = jnp.sum(
        head_view(out_grad).astype(jnp.float32) * head_view(attn_out).astype(jnp.float32), axis=2
    )
    pattern = live_pairs(own_pos, own_pos, segments, segments)
    query_acc, key_acc, value_acc = tile_terms(
        queries, out_grad, log_norm, row_delta, key_rows, value_rows, pattern
    )
    visit_q, visit_grad, visit_seg = (queries, out_grad, segments)
    visit_norm, visit_delta = (log_norm, row_delta)
    visit_acc = query_acc
    for offset in range(1, SEQ_DEVS):
        visit_q, visit_grad, visit_seg = pass_queries(visit_q, visit_grad, visit_seg)
        visit_acc, visit_norm, visit_delta = passed_along(
            (visit_acc, visit_norm, visit_delta), "ctx", -1
        )
        visit_pos = (block_index + offset) % chain_len * tok_rows + local_iota
        visit_pattern = live_pairs(visit_pos, own_pos, visit_seg, segments)
        query_add, key_add, value_add = tile_terms(
            visit_q, visit_grad, visit_norm, visit_delta, key_rows, value_rows, visit_pattern
        )
        visit_acc = visit_acc + query_add
        key_acc = key_acc + key_add
        value_acc = value_acc + value_add
    query_acc = passed_along(visit_acc.astype(jnp.bfloat16), "ctx", SEQ_DEVS - 1).astype(
        visit_acc.dtype
    )
    softmax_scale = HEAD_DIM ** (-0.5)
    return (
        (query_acc * softmax_scale).astype(jnp.bfloat16),
        (key_acc * softmax_scale).astype(jnp.bfloat16),
        value_acc.astype(jnp.bfloat16),
    )


def solution(mesh):
    placed = (
        P(("dp", "ctx"), None),
        P(("dp", "ctx"), None),
        P(("dp", "ctx"), None),
        P(("dp", "ctx"), None),
        P(("dp", "ctx"), None),
        P(("dp", "ctx"), None),
        P(("dp", "ctx")),
    )
    return jax.shard_map(
        on_device,
        mesh=mesh,
        in_specs=placed,
        out_specs=(P(("dp", "ctx"), None), P(("dp", "ctx"), None), P(("dp", "ctx"), None)),
        check_vma=False,
    )
```

profile of v0, /device:TPU:1, one launch (start us, length us, event | category | flops | bytes accessed | tf_op | source)
XLA Modules:
  0.0 278.0 jit_solution(16980175502845440860)
XLA Ops:
  0.7 2.1 collective-permute-start.1
  2.8 2.0 copy.225
  4.8 1.9 collective-permute-start.2
  8.5 6.9 %collective-permute-start.5 = (f32[128,16]{1,0:T(8,128)S(1)}, f32[128,16]{1,0:T(8,128)S(1)}, u32[]{:S(2)}, u32[]{:S(2)}) collective-permute-start(f32[128,16]{1,0:T(8,128)S(1)} %multiply_reduce_fusion), channel_id=1, source_target_pairs={{1,0},{2,1},{3,2},{4,3},{5,4},{6,5},{7,6},{8,7},{9,8},{10,9},{11,1... | collective-permute-start | bytes 24584 | tf_op jit(solution)/shard_map/ppermute | solution.py:27
  16.4 1.9 collective-permute-start.4
  18.4 1.9 collective-permute-start.7
  20.3 6.8 %collective-permute-done.7 = s32[128]{0:T(128)S(1)} collective-permute-done((s32[128]{0:T(128)S(1)}, s32[128]{0:T(128)S(1)}, u32[]{:S(2)}, u32[]{:S(2)}) %collective-permute-start.7) | collective-permute-done | bytes 544 | tf_op jit(solution)/shard_map/ppermute | solution.py:21
  29.1 2.9 %collective-permute-done.13 = s32[128]{0:T(128)S(1)} collective-permute-done((s32[128]{0:T(128)S(1)}, s32[128]{0:T(128)S(1)}, u32[]{:S(2)}, u32[]{:S(2)}) %collective-permute-start.13) | collective-permute-done | bytes 544 | tf_op jit(solution)/shard_map/ppermute | solution.py:21
  33.9 2.9 %collective-permute-done.19 = s32[128]{0:T(128)S(1)} collective-permute-done((s32[128]{0:T(128)S(1)}, s32[128]{0:T(128)S(1)}, u32[]{:S(2)}, u32[]{:S(2)}) %collective-permute-start.19) | collective-permute-done | bytes 544 | tf_op jit(solution)/shard_map/ppermute | solution.py:21
  36.9 1.9 collective-permute-start.25
  38.8 2.9 %collective-permute-done.25 = s32[128]{0:T(128)S(1)} collective-permute-done((s32[128]{0:T(128)S(1)}, s32[128]{0:T(128)S(1)}, u32[]{:S(2)}, u32[]{:S(2)}) %collective-permute-start.25) | collective-permute-done | bytes 544 | tf_op jit(solution)/shard_map/ppermute | solution.py:21
  43.7 2.9 %collective-permute-done.31 = s32[128]{0:T(128)S(1)} collective-permute-done((s32[128]{0:T(128)S(1)}, s32[128]{0:T(128)S(1)}, u32[]{:S(2)}, u32[]{:S(2)}) %collective-permute-start.31) | collective-permute-done | bytes 544 | tf_op jit(solution)/shard_map/ppermute | solution.py:21
  55.6 2.1 collective-permute-start.15
  57.6 2.4 collective-permute-start.23
  60.6 2.4 collective-permute-start.21
  63.0 2.8 %collective-permute-start.29 = (f32[128,16]{1,0:T(8,128)S(1)}, f32[128,16]{1,0:T(8,128)S(1)}, u32[]{:S(2)}, u32[]{:S(2)}) collective-permute-start(f32[128,16]{1,0:T(8,128)S(1)} %collective-permute-done.23), channel_id=1, source_target_pairs={{1,0},{2,1},{3,2},{4,3},{5,4},{6,5},{7,6},{8,7},{9,8},{10,9},{11,1... | collective-permute-start | bytes 24584 | tf_op jit(solution)/shard_map/ppermute | solution.py:27
  67.1 3.0 %collective-permute-start.27 = (f32[128,16]{0,1:T(8,128)S(1)}, f32[128,16]{0,1:T(8,128)}, u32[]{:S(2)}, u32[]{:S(2)}) collective-permute-start(f32[128,16]{0,1:T(8,128)S(1)} %collective-permute-done.21), channel_id=1, source_target_pairs={{1,0},{2,1},{3,2},{4,3},{5,4},{6,5},{7,6},{8,7},{9,8},{10,9},{11,1... | collective-permute-start | bytes 24584 | tf_op jit(solution)/shard_map/ppermute | solution.py:27
  71.6 2.5 fusion.100
  74.1 3.6 %collective-permute-start.33 = (f32[128,16]{0,1:T(8,128)}, f32[128,16]{0,1:T(8,128)S(1)}, u32[]{:S(2)}, u32[]{:S(2)}) collective-permute-start(f32[128,16]{0,1:T(8,128)} %collective-permute-done.27), channel_id=1, source_target_pairs={{1,0},{2,1},{3,2},{4,3},{5,4},{6,5},{7,6},{8,7},{9,8},{10,9},{11,1... | collective-permute-start | bytes 24584 | tf_op jit(solution)/shard_map/ppermute | solution.py:27
  79.6 3.8 %collective-permute-start = (f32[128,2048]{1,0:T(8,128)}, f32[128,2048]{1,0:T(8,128)}, u32[]{:S(2)}, u32[]{:S(2)}) collective-permute-start(f32[128,2048]{1,0:T(8,128)} %copy.138), channel_id=1, source_target_pairs={{1,0},{2,1},{3,2},{4,3},{5,4},{6,5},{7,6},{8,7},{9,8},{10,9},{11,1... | collective-permute-start | bytes 3145736 | tf_op jit(solution)/shard_map/ppermute | solution.py:27
  91.8 2.6 copy.147
  94.4 2.1 collective-permute-start.8
  96.5 1.9 collective-permute-start.10
  98.4 2.6 convolution_add_fusion.6
  101.0 2.6 convolution_add_fusion.13
  106.0 4.8 %collective-permute-done.10 = bf16[128,2048]{0,1:T(8,128)(2,1)S(1)} collective-permute-done((bf16[128,2048]{0,1:T(8,128)(2,1)}, bf16[128,2048]{0,1:T(8,128)(2,1)S(1)}, u32[]{:S(2)}, u32[]{:S(2)}) %collective-permute-start.10) | collective-permute-done | bytes 524320 | tf_op jit(solution)/shard_map/ppermute | solution.py:21
  113.2 2.5 copy.154
  115.7 2.0 collective-permute-start.14
  117.8 1.9 collective-permute-start.16
  119.7 2.6 convolution_add_fusion.5
  122.4 2.5 add.218
  127.4 4.8 %collective-permute-done.16 = bf16[128,2048]{0,1:T(8,128)(2,1)S(1)} collective-permute-done((bf16[128,2048]{0,1:T(8,128)(2,1)}, bf16[128,2048]{0,1:T(8,128)(2,1)S(1)}, u32[]{:S(2)}, u32[]{:S(2)}) %collective-permute-start.16) | collective-permute-done | bytes 524320 | tf_op jit(solution)/shard_map/ppermute | solution.py:21
  134.4 2.5 copy.161
  137.0 2.0 collective-permute-start.20
  139.0 1.9 collective-permute-start.22
  140.9 2.6 collective-permute-done.6
  149.8 4.8 %collective-permute-done.22 = bf16[128,2048]{0,1:T(8,128)(2,1)S(1)} collective-permute-done((bf16[128,2048]{0,1:T(8,128)(2,1)}, bf16[128,2048]{0,1:T(8,128)(2,1)S(1)}, u32[]{:S(2)}, u32[]{:S(2)}) %collective-permute-start.22) | collective-permute-done | bytes 524320 | tf_op jit(solution)/shard_map/ppermute | solution.py:21
  155.4 10.4 %collective-permute-done.12 = f32[128,2048]{1,0:T(8,128)S(1)} collective-permute-done((f32[128,2048]{1,0:T(8,128)S(1)}, f32[128,2048]{1,0:T(8,128)S(1)}, u32[]{:S(2)}, u32[]{:S(2)}) %collective-permute-start.12) | collective-permute-done | bytes 1048608 | tf_op jit(solution)/shard_map/ppermute | solution.py:27
  168.4 2.6 copy.168
  171.0 2.0 collective-permute-start.26
  173.1 1.9 collective-permute-start.28
  175.0 2.7 convolution_add_fusion.3
  179.2 7.9 %collective-permute-done.26 = bf16[128,2048]{0,1:T(8,128)(2,1)S(1)} collective-permute-done((bf16[128,2048]{0,1:T(8,128)(2,1)}, bf16[128,2048]{0,1:T(8,128)(2,1)S(1)}, u32[]{:S(2)}, u32[]{:S(2)}) %collective-permute-start.26) | collective-permute-done | bytes 524320 | tf_op jit(solution)/shard_map/ppermute | solution.py:21
  188.6 2.3 add.233
  194.9 2.5 copy.175
  197.4 2.0 collective-permute-start.32
  199.5 1.9 collective-permute-start.34
  201.4 2.7 convolution_add_fusion.2
  205.6 2.3 add.238
  207.9 3.1 %collective-permute-done.32 = bf16[128,2048]{0,1:T(8,128)(2,1)S(1)} collective-permute-done((bf16[128,2048]{0,1:T(8,128)(2,1)}, bf16[128,2048]{0,1:T(8,128)(2,1)S(1)}, u32[]{:S(2)}, u32[]{:S(2)}) %collective-permute-start.32) | collective-permute-done | bytes 524320 | tf_op jit(solution)/shard_map/ppermute | solution.py:21
  211.8 4.8 %collective-permute-done.34 = bf16[128,2048]{0,1:T(8,128)(2,1)S(1)} collective-permute-done((bf16[128,2048]{0,1:T(8,128)(2,1)}, bf16[128,2048]{0,1:T(8,128)(2,1)S(1)}, u32[]{:S(2)}, u32[]{:S(2)}) %collective-permute-start.34) | collective-permute-done | bytes 524320 | tf_op jit(solution)/shard_map/ppermute | solution.py:21
  218.8 2.5 copy.182
  221.4 2.0 collective-permute-start.38
  223.4 1.9 collective-permute-start.40
  225.3 2.7 convolution_add_fusion.1
  228.0 2.4 add.243
  234.2 4.8 %collective-permute-done.40 = bf16[128,2048]{0,1:T(8,128)(2,1)S(1)} collective-permute-done((bf16[128,2048]{0,1:T(8,128)(2,1)}, bf16[128,2048]{0,1:T(8,128)(2,1)S(1)}, u32[]{:S(2)}, u32[]{:S(2)}) %collective-permute-start.40) | collective-permute-done | bytes 524320 | tf_op jit(solution)/shard_map/ppermute | solution.py:21
  241.3 2.5 copy.189
  243.8 6.9 %collective-permute-done.36 = f32[128,2048]{1,0:T(8,128)} collective-permute-done((f32[128,2048]{1,0:T(8,128)}, f32[128,2048]{1,0:T(8,128)}, u32[]{:S(2)}, u32[]{:S(2)}) %collective-permute-start.36) | collective-permute-done | bytes 1048608 | tf_op jit(solution)/shard_map/ppermute | solution.py:27
  250.7 2.5 add_convert_fusion
  254.7 2.1 copy.201
  257.9 2.0 copy.202
  260.0 16.1 %collective-permute-done.42 = bf16[128,2048]{1,0:T(8,128)(2,1)} collective-permute-done((bf16[128,2048]{1,0:T(8,128)(2,1)}, bf16[128,2048]{1,0:T(8,128)(2,1)}, u32[]{:S(2)}, u32[]{:S(2)}) %collective-permute-start.42) | collective-permute-done | bytes 524320 | tf_op jit(solution)/shard_map/ppermute | solution.py:27
  276.1 1.9 multiply_convert_fusion
  (201 shorter events, 70.4 us)
Async XLA Ops:
  0.6 59.4 %copy-start = (bf16[128,2048]{1,0:T(8,128)(2,1)S(1)}, bf16[128,2048]{1,0:T(8,128)(2,1)}, u32[]{:S(2)}) copy-start(bf16[128,2048]{1,0:T(8,128)(2,1)} %param.9) | copy-start | bytes 1572868
  0.6 6.1 %copy-start.48 = (f32[128,16]{0,1:T(8,128)S(1)}, f32[128,16]{0,1:T(8,128)}, u32[]{:S(2)}) copy-start(f32[128,16]{0,1:T(8,128)} %param.12) | copy-start | bytes 24580
  0.7 6.2 %copy-start.23 = (bf16[128,2048]{1,0:T(8,128)(2,1)S(1)}, bf16[128,2048]{1,0:T(8,128)(2,1)}, u32[]{:S(2)}) copy-start(bf16[128,2048]{1,0:T(8,128)(2,1)} %param.11) | copy-start | bytes 1572868
  0.7 17.7 %collective-permute-start.1 = (s32[128]{0:T(128)}, s32[128]{0:T(128)S(1)}, u32[]{:S(2)}, u32[]{:S(2)}) collective-permute-start(s32[128]{0:T(128)} %param.13), channel_id=1, source_target_pairs={{1,0},{2,1},{3,2},{4,3},{5,4},{6,5},{7,6},{8,7},{9,8},{10,9},{11,1... | collective-permute-start | bytes 1544 | tf_op jit(solution)/shard_map/ppermute | solution.py:21
  4.8 81.5 %collective-permute-start.2 = (bf16[128,2048]{0,1:T(8,128)(2,1)}, bf16[128,2048]{0,1:T(8,128)(2,1)}, u32[]{:S(2)}, u32[]{:S(2)}) collective-permute-start(bf16[128,2048]{0,1:T(8,128)(2,1)} %copy.225), channel_id=1, source_target_pairs={{1,0},{2,1},{3,2},{4,3},{5,4},{6,5},{7,6},{8,7},{9,8},{10,9},{11,1... | collective-permute-start | bytes 1572872 | tf_op jit(solution)/shard_map/ppermute | solution.py:21
  6.7 45.7 %collective-permute-start.3 = (f32[128,16]{0,1:T(8,128)S(1)}, f32[128,16]{0,1:T(8,128)S(1)}, u32[]{:S(2)}, u32[]{:S(2)}) collective-permute-start(f32[128,16]{0,1:T(8,128)S(1)} %copy-done.48), channel_id=1, source_target_pairs={{1,0},{2,1},{3,2},{4,3},{5,4},{6,5},{7,6},{8,7},{9,8},{10,9},{11,1... | collective-permute-start | bytes 24584 | tf_op jit(solution)/shard_map/ppermute | solution.py:27
  8.5 41.1 %collective-permute-start.5 = (f32[128,16]{1,0:T(8,128)S(1)}, f32[128,16]{1,0:T(8,128)S(1)}, u32[]{:S(2)}, u32[]{:S(2)}) collective-permute-start(f32[128,16]{1,0:T(8,128)S(1)} %multiply_reduce_fusion), channel_id=1, source_target_pairs={{1,0},{2,1},{3,2},{4,3},{5,4},{6,5},{7,6},{8,7},{9,8},{10,9},{11,1... | collective-permute-start | bytes 24584 | tf_op jit(solution)/shard_map/ppermute | solution.py:27
  16.4 71.5 %collective-permute-start.4 = (bf16[128,2048]{0,1:T(8,128)(2,1)}, bf16[128,2048]{0,1:T(8,128)(2,1)S(1)}, u32[]{:S(2)}, u32[]{:S(2)}) collective-permute-start(bf16[128,2048]{0,1:T(8,128)(2,1)} %copy.142), channel_id=1, source_target_pairs={{1,0},{2,1},{3,2},{4,3},{5,4},{6,5},{7,6},{8,7},{9,8},{10,9},{11,1... | collective-permute-start | bytes 1572872 | tf_op jit(solution)/shard_map/ppermute | solution.py:21
  18.4 8.8 %collective-permute-start.7 = (s32[128]{0:T(128)S(1)}, s32[128]{0:T(128)S(1)}, u32[]{:S(2)}, u32[]{:S(2)}) collective-permute-start(s32[128]{0:T(128)S(1)} %collective-permute-done.1), channel_id=1, source_target_pairs={{1,0},{2,1},{3,2},{4,3},{5,4},{6,5},{7,6},{8,7},{9,8},{10,9},{11,1... | collective-permute-start | bytes 1544 | tf_op jit(solution)/shard_map/ppermute | solution.py:21
  27.2 4.8 %collective-permute-start.13 = (s32[128]{0:T(128)S(1)}, s32[128]{0:T(128)S(1)}, u32[]{:S(2)}, u32[]{:S(2)}) collective-permute-start(s32[128]{0:T(128)S(1)} %collective-permute-done.7), channel_id=1, source_target_pairs={{1,0},{2,1},{3,2},{4,3},{5,4},{6,5},{7,6},{8,7},{9,8},{10,9},{11,1... | collective-permute-start | bytes 1544 | tf_op jit(solution)/shard_map/ppermute | solution.py:21
  32.0 4.8 %collective-permute-start.19 = (s32[128]{0:T(128)S(1)}, s32[128]{0:T(128)S(1)}, u32[]{:S(2)}, u32[]{:S(2)}) collective-permute-start(s32[128]{0:T(128)S(1)} %collective-permute-done.13), channel_id=1, source_target_pairs={{1,0},{2,1},{3,2},{4,3},{5,4},{6,5},{7,6},{8,7},{9,8},{10,9},{11,1... | collective-permute-start | bytes 1544 | tf_op jit(solution)/shard_map/ppermute | solution.py:21
  36.9 4.8 %collective-permute-start.25 = (s32[128]{0:T(128)S(1)}, s32[128]{0:T(128)S(1)}, u32[]{:S(2)}, u32[]{:S(2)}) collective-permute-start(s32[128]{0:T(128)S(1)} %collective-permute-done.19), channel_id=1, source_target_pairs={{1,0},{2,1},{3,2},{4,3},{5,4},{6,5},{7,6},{8,7},{9,8},{10,9},{11,1... | collective-permute-start | bytes 1544 | tf_op jit(solution)/shard_map/ppermute | solution.py:21
  41.7 4.8 %collective-permute-start.31 = (s32[128]{0:T(128)S(1)}, s32[128]{0:T(128)S(1)}, u32[]{:S(2)}, u32[]{:S(2)}) collective-permute-start(s32[128]{0:T(128)S(1)} %collective-permute-done.25), channel_id=1, source_target_pairs={{1,0},{2,1},{3,2},{4,3},{5,4},{6,5},{7,6},{8,7},{9,8},{10,9},{11,1... | collective-permute-start | bytes 1544 | tf_op jit(solution)/shard_map/ppermute | solution.py:21
  43.6 5.4 %copy-start.1 = (bf16[128,2048]{1,0:T(8,128)(2,1)S(1)}, bf16[128,2048]{1,0:T(8,128)(2,1)}, u32[]{:S(2)}) copy-start(bf16[128,2048]{1,0:T(8,128)(2,1)} %param.8) | copy-start | bytes 1572868
  46.6 4.8 %collective-permute-start.37 = (s32[128]{0:T(128)S(1)}, s32[128]{0:T(128)S(1)}, u32[]{:S(2)}, u32[]{:S(2)}) collective-permute-start(s32[128]{0:T(128)S(1)} %collective-permute-done.31), channel_id=1, source_target_pairs={{1,0},{2,1},{3,2},{4,3},{5,4},{6,5},{7,6},{8,7},{9,8},{10,9},{11,1... | collective-permute-start | bytes 1544 | tf_op jit(solution)/shard_map/ppermute | solution.py:21
  49.6 3.7 %collective-permute-start.11 = (f32[128,16]{1,0:T(8,128)S(1)}, f32[128,16]{1,0:T(8,128)S(1)}, u32[]{:S(2)}, u32[]{:S(2)}) collective-permute-start(f32[128,16]{1,0:T(8,128)S(1)} %collective-permute-done.5), channel_id=1, source_target_pairs={{1,0},{2,1},{3,2},{4,3},{5,4},{6,5},{7,6},{8,7},{9,8},{10,9},{11,1... | collective-permute-start | bytes 24584 | tf_op jit(solution)/shard_map/ppermute | solution.py:27
  52.4 3.1 %collective-permute-start.9 = (f32[128,16]{0,1:T(8,128)S(1)}, f32[128,16]{0,1:T(8,128)S(1)}, u32[]{:S(2)}, u32[]{:S(2)}) collective-permute-start(f32[128,16]{0,1:T(8,128)S(1)} %collective-permute-done.3), channel_id=1, source_target_pairs={{1,0},{2,1},{3,2},{4,3},{5,4},{6,5},{7,6},{8,7},{9,8},{10,9},{11,1... | collective-permute-start | bytes 24584 | tf_op jit(solution)/shard_map/ppermute | solution.py:27
  53.4 4.3 %collective-permute-start.17 = (f32[128,16]{1,0:T(8,128)S(1)}, f32[128,16]{1,0:T(8,128)S(1)}, u32[]{:S(2)}, u32[]{:S(2)}) collective-permute-start(f32[128,16]{1,0:T(8,128)S(1)} %collective-permute-done.11), channel_id=1, source_target_pairs={{1,0},{2,1},{3,2},{4,3},{5,4},{6,5},{7,6},{8,7},{9,8},{10,9},{11,1... | collective-permute-start | bytes 24584 | tf_op jit(solution)/shard_map/ppermute | solution.py:27
  55.5 5.1 %copy-start.45 = (f32[128,16]{0,1:T(8,128)}, f32[128,16]{0,1:T(8,128)S(1)}, u32[]{:S(2)}) copy-start(f32[128,16]{0,1:T(8,128)S(1)} %collective-permute-done.9) | copy-start | bytes 24580
  55.6 5.1 %collective-permute-start.15 = (f32[128,16]{0,1:T(8,128)S(1)}, f32[128,16]{0,1:T(8,128)S(1)}, u32[]{:S(2)}, u32[]{:S(2)}) collective-permute-start(f32[128,16]{0,1:T(8,128)S(1)} %collective-permute-done.9), channel_id=1, source_target_pairs={{1,0},{2,1},{3,2},{4,3},{5,4},{6,5},{7,6},{8,7},{9,8},{10,9},{11,1... | collective-permute-start | bytes 24584 | tf_op jit(solution)/shard_map/ppermute | solution.py:27
  57.6 5.4 %collective-permute-start.23 = (f32[128,16]{1,0:T(8,128)S(1)}, f32[128,16]{1,0:T(8,128)S(1)}, u32[]{:S(2)}, u32[]{:S(2)}) collective-permute-start(f32[128,16]{1,0:T(8,128)S(1)} %collective-permute-done.17), channel_id=1, source_target_pairs={{1,0},{2,1},{3,2},{4,3},{5,4},{6,5},{7,6},{8,7},{9,8},{10,9},{11,1... | collective-permute-start | bytes 24584 | tf_op jit(solution)/shard_map/ppermute | solution.py:27
  60.6 6.4 %copy-start.43 = (f32[128,16]{0,1:T(8,128)}, f32[128,16]{0,1:T(8,128)S(1)}, u32[]{:S(2)}) copy-start(f32[128,16]{0,1:T(8,128)S(1)} %collective-permute-done.15) | copy-start | bytes 24580
  60.6 6.4 %collective-permute-start.21 = (f32[128,16]{0,1:T(8,128)S(1)}, f32[128,16]{0,1:T(8,128)S(1)}, u32[]{:S(2)}, u32[]{:S(2)}) collective-permute-start(f32[128,16]{0,1:T(8,128)S(1)} %collective-permute-done.15), channel_id=1, source_target_pairs={{1,0},{2,1},{3,2},{4,3},{5,4},{6,5},{7,6},{8,7},{9,8},{10,9},{11,1... | collective-permute-start | bytes 24584 | tf_op jit(solution)/shard_map/ppermute | solution.py:27
  63.0 7.0 %collective-permute-start.29 = (f32[128,16]{1,0:T(8,128)S(1)}, f32[128,16]{1,0:T(8,128)S(1)}, u32[]{:S(2)}, u32[]{:S(2)}) collective-permute-start(f32[128,16]{1,0:T(8,128)S(1)} %collective-permute-done.23), channel_id=1, source_target_pairs={{1,0},{2,1},{3,2},{4,3},{5,4},{6,5},{7,6},{8,7},{9,8},{10,9},{11,1... | collective-permute-start | bytes 24584 | tf_op jit(solution)/shard_map/ppermute | solution.py:27
  67.1 7.0 %copy-start.41 = (f32[128,16]{0,1:T(8,128)}, f32[128,16]{0,1:T(8,128)S(1)}, u32[]{:S(2)}) copy-start(f32[128,16]{0,1:T(8,128)S(1)} %collective-permute-done.21) | copy-start | bytes 24580
  67.1 7.0 %collective-permute-start.27 = (f32[128,16]{0,1:T(8,128)S(1)}, f32[128,16]{0,1:T(8,128)}, u32[]{:S(2)}, u32[]{:S(2)}) collective-permute-start(f32[128,16]{0,1:T(8,128)S(1)} %collective-permute-done.21), channel_id=1, source_target_pairs={{1,0},{2,1},{3,2},{4,3},{5,4},{6,5},{7,6},{8,7},{9,8},{10,9},{11,1... | collective-permute-start | bytes 24584 | tf_op jit(solution)/shard_map/ppermute | solution.py:27
  70.0 4.1 %copy-start.39 = (f32[128,16]{1,0:T(8,128)}, f32[128,16]{1,0:T(8,128)S(1)}, u32[]{:S(2)}) copy-start(f32[128,16]{1,0:T(8,128)S(1)} %collective-permute-done.29) | copy-start | bytes 24580
  70.0 7.7 %collective-permute-start.35 = (f32[128,16]{1,0:T(8,128)S(1)}, f32[128,16]{1,0:T(8,128)}, u32[]{:S(2)}, u32[]{:S(2)}) collective-permute-start(f32[128,16]{1,0:T(8,128)S(1)} %collective-permute-done.29), channel_id=1, source_target_pairs={{1,0},{2,1},{3,2},{4,3},{5,4},{6,5},{7,6},{8,7},{9,8},{10,9},{11,1... | collective-permute-start | bytes 24584 | tf_op jit(solution)/shard_map/ppermute | solution.py:27
  74.1 11.2 %collective-permute-start.33 = (f32[128,16]{0,1:T(8,128)}, f32[128,16]{0,1:T(8,128)S(1)}, u32[]{:S(2)}, u32[]{:S(2)}) collective-permute-start(f32[128,16]{0,1:T(8,128)} %collective-permute-done.27), channel_id=1, source_target_pairs={{1,0},{2,1},{3,2},{4,3},{5,4},{6,5},{7,6},{8,7},{9,8},{10,9},{11,1... | collective-permute-start | bytes 24584 | tf_op jit(solution)/shard_map/ppermute | solution.py:27
  77.7 7.7 %collective-permute-start.41 = (f32[128,16]{1,0:T(8,128)}, f32[128,16]{1,0:T(8,128)}, u32[]{:S(2)}, u32[]{:S(2)}) collective-permute-start(f32[128,16]{1,0:T(8,128)} %collective-permute-done.35), channel_id=1, source_target_pairs={{1,0},{2,1},{3,2},{4,3},{5,4},{6,5},{7,6},{8,7},{9,8},{10,9},{11,1... | collective-permute-start | bytes 24584 | tf_op jit(solution)/shard_map/ppermute | solution.py:27
  79.6 42.8 %collective-permute-start = (f32[128,2048]{1,0:T(8,128)}, f32[128,2048]{1,0:T(8,128)}, u32[]{:S(2)}, u32[]{:S(2)}) collective-permute-start(f32[128,2048]{1,0:T(8,128)} %copy.138), channel_id=1, source_target_pairs={{1,0},{2,1},{3,2},{4,3},{5,4},{6,5},{7,6},{8,7},{9,8},{10,9},{11,1... | collective-permute-start | bytes 3145736 | tf_op jit(solution)/shard_map/ppermute | solution.py:27
  85.3 146.6 %collective-permute-start.39 = (f32[128,16]{0,1:T(8,128)S(1)}, f32[128,16]{0,1:T(8,128)S(1)}, u32[]{:S(2)}, u32[]{:S(2)}) collective-permute-start(f32[128,16]{0,1:T(8,128)S(1)} %collective-permute-done.33), channel_id=1, source_target_pairs={{1,0},{2,1},{3,2},{4,3},{5,4},{6,5},{7,6},{8,7},{9,8},{10,9},{11,1... | collective-permute-start | bytes 24584 | tf_op jit(solution)/shard_map/ppermute | solution.py:27
  94.4 6.6 %copy-start.9 = (f32[16,128,128]{2,1,0:T(8,128)S(1)}, f32[16,128,128]{2,1,0:T(8,128)}, u32[]{:S(2)}) copy-start(f32[16,128,128]{2,1,0:T(8,128)} %fusion.100) | copy-start | bytes 3145732
  94.4 10.8 %collective-permute-start.8 = (bf16[128,2048]{0,1:T(8,128)(2,1)}, bf16[128,2048]{0,1:T(8,128)(2,1)S(1)}, u32[]{:S(2)}, u32[]{:S(2)}) collective-permute-start(bf16[128,2048]{0,1:T(8,128)(2,1)} %collective-permute-done.2), channel_id=1, source_target_pairs={{1,0},{2,1},{3,2},{4,3},{5,4},{6,5},{7,6},{8,7},{9,8},{10,9},{11,1... | collective-permute-start | bytes 1572872 | tf_op jit(solution)/shard_map/ppermute | solution.py:21
  96.5 14.4 %collective-permute-start.10 = (bf16[128,2048]{0,1:T(8,128)(2,1)}, bf16[128,2048]{0,1:T(8,128)(2,1)S(1)}, u32[]{:S(2)}, u32[]{:S(2)}) collective-permute-start(bf16[128,2048]{0,1:T(8,128)(2,1)} %copy-done.16), channel_id=1, source_target_pairs={{1,0},{2,1},{3,2},{4,3},{5,4},{6,5},{7,6},{8,7},{9,8},{10,9},{11,1... | collective-permute-start | bytes 1572872 | tf_op jit(solution)/shard_map/ppermute | solution.py:21
  101.0 4.2 %copy-start.46 = (f32[128,16]{0,1:T(8,128)S(1)}, f32[128,16]{0,1:T(8,128)}, u32[]{:S(2)}) copy-start(f32[128,16]{0,1:T(8,128)} %copy-done.45) | copy-start | bytes 24580
  115.7 6.6 %copy-start.10 = (f32[128,2048]{1,0:T(8,128)S(1)}, f32[128,2048]{1,0:T(8,128)}, u32[]{:S(2)}) copy-start(f32[128,2048]{1,0:T(8,128)} %copy.147) | copy-start | bytes 3145732
  115.7 10.8 %collective-permute-start.14 = (bf16[128,2048]{0,1:T(8,128)(2,1)}, bf16[128,2048]{0,1:T(8,128)(2,1)S(1)}, u32[]{:S(2)}, u32[]{:S(2)}) collective-permute-start(bf16[128,2048]{0,1:T(8,128)(2,1)} %copy-done.36), channel_id=1, source_target_pairs={{1,0},{2,1},{3,2},{4,3},{5,4},{6,5},{7,6},{8,7},{9,8},{10,9},{11,1... | collective-permute-start | bytes 1572872 | tf_op jit(solution)/shard_map/ppermute | solution.py:21
  117.8 14.4 %collective-permute-start.16 = (bf16[128,2048]{0,1:T(8,128)(2,1)}, bf16[128,2048]{0,1:T(8,128)(2,1)S(1)}, u32[]{:S(2)}, u32[]{:S(2)}) collective-permute-start(bf16[128,2048]{0,1:T(8,128)(2,1)} %copy-done.22), channel_id=1, source_target_pairs={{1,0},{2,1},{3,2},{4,3},{5,4},{6,5},{7,6},{8,7},{9,8},{10,9},{11,1... | collective-permute-start | bytes 1572872 | tf_op jit(solution)/shard_map/ppermute | solution.py:21
  124.8 18.7 %collective-permute-start.6 = (f32[128,2048]{1,0:T(8,128)}, f32[128,2048]{1,0:T(8,128)}, u32[]{:S(2)}, u32[]{:S(2)}) collective-permute-start(f32[128,2048]{1,0:T(8,128)} %add.218), channel_id=1, source_target_pairs={{1,0},{2,1},{3,2},{4,3},{5,4},{6,5},{7,6},{8,7},{9,8},{10,9},{11,1... | collective-permute-start | bytes 3145736 | tf_op jit(solution)/shard_map/ppermute | solution.py:27
  137.0 8.3 %copy-start.3 = (f32[16,128,128]{1,2,0:T(8,128)S(1)}, f32[16,128,128]{1,2,0:T(8,128)}, u32[]{:S(2)}) copy-start(f32[16,128,128]{1,2,0:T(8,128)} %convolution_add_fusion.5) | copy-start | bytes 3145732
  137.0 8.3 %copy-start.20 = (bf16[128,2048]{0,1:T(8,128)(2,1)S(1)}, bf16[128,2048]{0,1:T(8,128)(2,1)}, u32[]{:S(2)}) copy-start(bf16[128,2048]{0,1:T(8,128)(2,1)} %copy-done.19) | copy-start | bytes 1572868
  137.0 12.1 %collective-permute-start.20 = (bf16[128,2048]{0,1:T(8,128)(2,1)}, bf16[128,2048]{0,1:T(8,128)(2,1)S(1)}, u32[]{:S(2)}, u32[]{:S(2)}) collective-permute-start(bf16[128,2048]{0,1:T(8,128)(2,1)} %copy-done.30), channel_id=1, source_target_pairs={{1,0},{2,1},{3,2},{4,3},{5,4},{6,5},{7,6},{8,7},{9,8},{10,9},{11,1... | collective-permute-start | bytes 1572872 | tf_op jit(solution)/shard_map/ppermute | solution.py:21
  139.0 15.6 %collective-permute-start.22 = (bf16[128,2048]{0,1:T(8,128)(2,1)}, bf16[128,2048]{0,1:T(8,128)(2,1)S(1)}, u32[]{:S(2)}, u32[]{:S(2)}) collective-permute-start(bf16[128,2048]{0,1:T(8,128)(2,1)} %copy-done.19), channel_id=1, source_target_pairs={{1,0},{2,1},{3,2},{4,3},{5,4},{6,5},{7,6},{8,7},{9,8},{10,9},{11,1... | collective-permute-start | bytes 1572872 | tf_op jit(solution)/shard_map/ppermute | solution.py:21
  145.2 20.7 %collective-permute-start.12 = (f32[128,2048]{1,0:T(8,128)S(1)}, f32[128,2048]{1,0:T(8,128)S(1)}, u32[]{:S(2)}, u32[]{:S(2)}) collective-permute-start(f32[128,2048]{1,0:T(8,128)S(1)} %add.223), channel_id=1, source_target_pairs={{1,0},{2,1},{3,2},{4,3},{5,4},{6,5},{7,6},{8,7},{9,8},{10,9},{11,1... | collective-permute-start | bytes 3145736 | tf_op jit(solution)/shard_map/ppermute | solution.py:27
  154.7 11.2 %copy-start.11 = (f32[128,2048]{1,0:T(8,128)S(1)}, f32[128,2048]{1,0:T(8,128)}, u32[]{:S(2)}) copy-start(f32[128,2048]{1,0:T(8,128)} %copy.161) | copy-start | bytes 3145732
  167.0 21.6 %collective-permute-start.18 = (f32[128,2048]{1,0:T(8,128)}, f32[128,2048]{1,0:T(8,128)}, u32[]{:S(2)}, u32[]{:S(2)}) collective-permute-start(f32[128,2048]{1,0:T(8,128)} %add.228), channel_id=1, source_target_pairs={{1,0},{2,1},{3,2},{4,3},{5,4},{6,5},{7,6},{8,7},{9,8},{10,9},{11,1... | collective-permute-start | bytes 3145736 | tf_op jit(solution)/shard_map/ppermute | solution.py:27
  171.0 6.7 %copy-start.7 = (f32[16,128,128]{2,1,0:T(8,128)S(1)}, f32[16,128,128]{2,1,0:T(8,128)}, u32[]{:S(2)}) copy-start(f32[16,128,128]{2,1,0:T(8,128)} %convolution_add_fusion.11) | copy-start | bytes 3145732
  171.0 6.7 %copy-start.33 = (bf16[128,2048]{0,1:T(8,128)(2,1)S(1)}, bf16[128,2048]{0,1:T(8,128)(2,1)}, u32[]{:S(2)}) copy-start(bf16[128,2048]{0,1:T(8,128)(2,1)} %copy-done.32) | copy-start | bytes 1572868
  171.0 16.0 %collective-permute-start.26 = (bf16[128,2048]{0,1:T(8,128)(2,1)}, bf16[128,2048]{0,1:T(8,128)(2,1)S(1)}, u32[]{:S(2)}, u32[]{:S(2)}) collective-permute-start(bf16[128,2048]{0,1:T(8,128)(2,1)} %copy-done.32), channel_id=1, source_target_pairs={{1,0},{2,1},{3,2},{4,3},{5,4},{6,5},{7,6},{8,7},{9,8},{10,9},{11,1... | collective-permute-start | bytes 1572872 | tf_op jit(solution)/shard_map/ppermute | solution.py:21
  173.1 19.6 %collective-permute-start.28 = (bf16[128,2048]{0,1:T(8,128)(2,1)}, bf16[128,2048]{0,1:T(8,128)(2,1)S(1)}, u32[]{:S(2)}, u32[]{:S(2)}) collective-permute-start(bf16[128,2048]{0,1:T(8,128)(2,1)} %copy-done.17), channel_id=1, source_target_pairs={{1,0},{2,1},{3,2},{4,3},{5,4},{6,5},{7,6},{8,7},{9,8},{10,9},{11,1... | collective-permute-start | bytes 1572872 | tf_op jit(solution)/shard_map/ppermute | solution.py:21
  190.9 14.6 %collective-permute-start.24 = (f32[128,2048]{1,0:T(8,128)}, f32[128,2048]{1,0:T(8,128)}, u32[]{:S(2)}, u32[]{:S(2)}) collective-permute-start(f32[128,2048]{1,0:T(8,128)} %add.233), channel_id=1, source_target_pairs={{1,0},{2,1},{3,2},{4,3},{5,4},{6,5},{7,6},{8,7},{9,8},{10,9},{11,1... | collective-permute-start | bytes 3145736 | tf_op jit(solution)/shard_map/ppermute | solution.py:27
  197.4 6.7 %copy-start.8 = (f32[16,128,128]{2,1,0:T(8,128)S(1)}, f32[16,128,128]{2,1,0:T(8,128)}, u32[]{:S(2)}) copy-start(f32[16,128,128]{2,1,0:T(8,128)} %convolution_add_fusion.10) | copy-start | bytes 3145732
  197.4 6.7 %copy-start.35 = (bf16[128,2048]{0,1:T(8,128)(2,1)S(1)}, bf16[128,2048]{0,1:T(8,128)(2,1)}, u32[]{:S(2)}) copy-start(bf16[128,2048]{0,1:T(8,128)(2,1)} %copy-done.34) | copy-start | bytes 1572868
  197.4 13.6 %collective-permute-start.32 = (bf16[128,2048]{0,1:T(8,128)(2,1)}, bf16[128,2048]{0,1:T(8,128)(2,1)S(1)}, u32[]{:S(2)}, u32[]{:S(2)}) collective-permute-start(bf16[128,2048]{0,1:T(8,128)(2,1)} %copy-done.34), channel_id=1, source_target_pairs={{1,0},{2,1},{3,2},{4,3},{5,4},{6,5},{7,6},{8,7},{9,8},{10,9},{11,1... | collective-permute-start | bytes 1572872 | tf_op jit(solution)/shard_map/ppermute | solution.py:21
  199.5 17.1 %collective-permute-start.34 = (bf16[128,2048]{0,1:T(8,128)(2,1)}, bf16[128,2048]{0,1:T(8,128)(2,1)S(1)}, u32[]{:S(2)}, u32[]{:S(2)}) collective-permute-start(bf16[128,2048]{0,1:T(8,128)(2,1)} %copy-done.21), channel_id=1, source_target_pairs={{1,0},{2,1},{3,2},{4,3},{5,4},{6,5},{7,6},{8,7},{9,8},{10,9},{11,1... | collective-permute-start | bytes 1572872 | tf_op jit(solution)/shard_map/ppermute | solution.py:21
  207.9 20.1 %collective-permute-start.30 = (f32[128,2048]{1,0:T(8,128)}, f32[128,2048]{1,0:T(8,128)}, u32[]{:S(2)}, u32[]{:S(2)}) collective-permute-start(f32[128,2048]{1,0:T(8,128)} %add.238), channel_id=1, source_target_pairs={{1,0},{2,1},{3,2},{4,3},{5,4},{6,5},{7,6},{8,7},{9,8},{10,9},{11,1... | collective-permute-start | bytes 3145736 | tf_op jit(solution)/shard_map/ppermute | solution.py:27
  221.4 6.7 %copy-start.15 = (f32[128,2048]{1,0:T(8,128)S(1)}, f32[128,2048]{1,0:T(8,128)}, u32[]{:S(2)}) copy-start(f32[128,2048]{1,0:T(8,128)} %copy.182) | copy-start | bytes 3145732
  221.4 12.1 %collective-permute-start.38 = (bf16[128,2048]{0,1:T(8,128)(2,1)}, bf16[128,2048]{0,1:T(8,128)(2,1)S(1)}, u32[]{:S(2)}, u32[]{:S(2)}) collective-permute-start(bf16[128,2048]{0,1:T(8,128)(2,1)} %copy-done.28), channel_id=1, source_target_pairs={{1,0},{2,1},{3,2},{4,3},{5,4},{6,5},{7,6},{8,7},{9,8},{10,9},{11,1... | collective-permute-start | bytes 1572872 | tf_op jit(solution)/shard_map/ppermute | solution.py:21
  223.4 15.7 %collective-permute-start.40 = (bf16[128,2048]{0,1:T(8,128)(2,1)}, bf16[128,2048]{0,1:T(8,128)(2,1)S(1)}, u32[]{:S(2)}, u32[]{:S(2)}) collective-permute-start(bf16[128,2048]{0,1:T(8,128)(2,1)} %copy-done.18), channel_id=1, source_target_pairs={{1,0},{2,1},{3,2},{4,3},{5,4},{6,5},{7,6},{8,7},{9,8},{10,9},{11,1... | collective-permute-start | bytes 1572872 | tf_op jit(solution)/shard_map/ppermute | solution.py:21
  230.4 20.3 %collective-permute-start.36 = (f32[128,2048]{1,0:T(8,128)}, f32[128,2048]{1,0:T(8,128)}, u32[]{:S(2)}, u32[]{:S(2)}) collective-permute-start(f32[128,2048]{1,0:T(8,128)} %add.243), channel_id=1, source_target_pairs={{1,0},{2,1},{3,2},{4,3},{5,4},{6,5},{7,6},{8,7},{9,8},{10,9},{11,1... | collective-permute-start | bytes 3145736 | tf_op jit(solution)/shard_map/ppermute | solution.py:27
  243.8 9.3 %copy-start.12 = (f32[16,128,128]{2,1,0:T(8,128)S(1)}, f32[16,128,128]{2,1,0:T(8,128)}, u32[]{:S(2)}) copy-start(f32[16,128,128]{2,1,0:T(8,128)} %convolution_add_fusion.8) | copy-start | bytes 3145732
  243.8 9.3 %copy-start.27 = (bf16[128,2048]{0,1:T(8,128)(2,1)S(1)}, bf16[128,2048]{0,1:T(8,128)(2,1)}, u32[]{:S(2)}) copy-start(bf16[128,2048]{0,1:T(8,128)(2,1)} %copy-done.26) | copy-start | bytes 1572868
  253.2 22.9 %collective-permute-start.42 = (bf16[128,2048]{1,0:T(8,128)(2,1)}, bf16[128,2048]{1,0:T(8,128)(2,1)}, u32[]{:S(2)}, u32[]{:S(2)}) collective-permute-start(bf16[128,2048]{1,0:T(8,128)(2,1)} %add_convert_fusion), channel_id=1, source_target_pairs={{9,0},{10,1},{11,2},{12,3},{13,4},{14,5},{15,6},{0,7},{1,8},{2,9},... | collective-permute-start | bytes 1572872 | tf_op jit(solution)/shard_map/ppermute | solution.py:27
  (28 other events, 38.7 us)
where the time goes:
time: 280 us; the launch traced here: 278 us
  waiting for transfers between devices  98.6 us (35%)
  starting transfers between devices  70 us (25%)
  matrix products  54.7 us (20%)
  local copies, waits for them, and re-layouts  35.8 us (13%)
  other arithmetic  17.5 us (6%)
    ppermute x21, waiting for transfers between devices, from_behind(): return lax.ppermute(value, axis, pairs)  61.2 us
    ppermute x21, starting transfers between devices, from_behind(): return lax.ppermute(value, axis, pairs)  41.2 us
    ppermute x22, waiting for transfers between devices, passed_along(): return lax.ppermute(block, axis, route)  37.5 us
    ppermute x22, starting transfers between devices, passed_along(): return lax.ppermute(block, axis, route)  28.8 us
    reshape x8, local copies, waits for them, and re-layouts, tile_terms(): results.append(query_add.reshape(queries.shape[0], -1))  19.1 us
    dot_general x8, matrix products, tile_terms(): jnp.einsum('hqk,qhd->khd', attn_prob.astype(jnp.bfloat16), head_view(out_...  17 us
    dot_general x8, matrix products, tile_terms(): jnp.einsum('hqk,qhd->khd', score_low, head_view(queries), preferred_eleme...  13.1 us
    add x6, other arithmetic, on_device(): visit_acc = visit_acc + query_add  12.3 us
  transfers between devices with their start and end apart: 43, of which 24 were waited for; matrix products, arithmetic and copies ran while one was open for 35% of the time, Pallas kernels for 0%

commit v1 on v0

v1 whole, which is shorter than its diff:
```python
import functools

import jax
import jax.numpy as jnp
from jax import lax
from jax.experimental import pallas as pl
from jax.experimental.pallas import tpu as pltpu
from jax.sharding import PartitionSpec as P

HEAD_DIM = 128
SEQ_DEVS = 8
GROUP = 4
LOG2E = 1.4426950408889634
MESH = pl.DeviceIdType.MESH
SCALE = HEAD_DIM ** (-0.5)


def dot(a, b, a_dim, b_dim):
    return lax.dot_general(a, b, (((a_dim,), (b_dim,)), ((), ())), preferred_element_type=jnp.float32)


def kernel(
    chain_len,
    q_ref, k_ref, v_ref, o_ref, g_ref, ln_ref, seg_ref,
    dq_ref, dk_ref, dv_ref,
    stat_send, visit, stat, keys, values, key_seg, dk_acc, dv_acc, dq_acc,
    dq_send, dq_recv, out_send,
    in_ssem, in_rsem, hop_ssem, hop_rsem, dq_ssem, dq_rsem, out_ssem, out_rsem,
):
    tok = q_ref.shape[0]
    cols = q_ref.shape[1] // GROUP
    heads = cols // HEAD_DIM
    me = lax.axis_index("ctx")
    layer = me // GROUP
    place = me % GROUP
    layers = chain_len // GROUP
    base = layer * GROUP
    flip = place + 1 - 2 * (place % 2)
    order = [place, flip, (place + 2) % GROUP, (flip + 2) % GROUP]
    prev1, prev2 = layer >= 1, layer >= 2
    next1, next2 = layer <= layers - 2, layer <= layers - 3

    def part(p):
        return pl.ds(pl.multiple_of(p * cols, cols), cols)

    def rows_of(b):
        return pl.ds(pl.multiple_of(b * tok, tok), tok)

    def copy(src, dst, ssem, rsem, to):
        return pltpu.make_async_remote_copy(
            src_ref=src, dst_ref=dst, send_sem=ssem, recv_sem=rsem,
            device_id={"ctx": to}, device_id_type=MESH,
        )

    barrier = pltpu.get_barrier_semaphore()

    def greet(to):
        pl.semaphore_signal(barrier, inc=1, device_id={"ctx": to}, device_id_type=MESH)

    for r in range(1, GROUP):
        greet(base + order[r])
    for there, to in ((prev1, me - GROUP), (prev2, me - 2 * GROUP), (next1, me + GROUP), (next2, me + 2 * GROUP)):
        pl.when(there)(functools.partial(greet, to))

    visit[0, place, 0] = q_ref[:, part(place)]
    visit[0, place, 1] = g_ref[:, part(place)]
    keys[rows_of(place), :] = k_ref[:, part(place)]
    values[rows_of(place), :] = v_ref[:, part(place)]

    lane = lax.broadcasted_iota(jnp.int32, (tok, 128), 1)
    table = jnp.zeros((tok, 128), jnp.float32)
    for h in range(GROUP * heads):
        here = slice(h * HEAD_DIM, (h + 1) * HEAD_DIM)
        delta = jnp.sum(g_ref[:, here].astype(jnp.float32) * o_ref[:, here].astype(jnp.float32), axis=1, keepdims=True)
        at = (h // heads) * 16 + h % heads
        table = jnp.where(lane == at, delta, table)
        table = jnp.where(lane == at + heads, ln_ref[:, h : h + 1] * LOG2E, table)
    table = table.T
    seg_rows = jnp.broadcast_to(seg_ref[...].astype(jnp.float32), (8, tok))
    for p in range(GROUP):
        stat_send[p, 0:8, :] = table[16 * p : 16 * p + 8, :]
        stat_send[p, 8:16, :] = seg_rows
    stat[0, place] = stat_send[place]
    dk_acc[...] = jnp.zeros_like(dk_acc)
    dv_acc[...] = jnp.zeros_like(dv_acc)

    partners = 3 + prev1.astype(jnp.int32) + prev2.astype(jnp.int32) + next1.astype(jnp.int32) + next2.astype(jnp.int32)
    pl.semaphore_wait(barrier, partners)

    def in_copy(a, r, sending):
        p = order[r]
        at = place if sending else p
        src = (q_ref.at[:, part(p)], g_ref.at[:, part(p)], stat_send.at[p], k_ref.at[:, part(p)], v_ref.at[:, part(p)])[a]
        dst = (visit.at[0, at, 0], visit.at[0, at, 1], stat.at[0, at], keys.at[rows_of(at)], values.at[rows_of(at)])[a]
        return copy(src, dst, in_ssem.at[a, r], in_rsem.at[a, r], base + p)

    def hop_copies(hop, b):
        to = me - GROUP
        return (
            copy(visit.at[hop, b], visit.at[hop + 1, b], hop_ssem.at[hop, 0, b], hop_rsem.at[hop, 0, b], to),
            copy(stat.at[hop, b], stat.at[hop + 1, b], hop_ssem.at[hop, 1, b], hop_rsem.at[hop, 1, b], to),
        )

    def dq_copy(d, b):
        return copy(dq_send.at[d, b], dq_recv.at[d, b], dq_ssem.at[d, b], dq_rsem.at[d, b], me + (d + 1) * GROUP)

    def out_copy(a, r, sending):
        ref = (dq_ref, dk_ref, dv_ref)[a]
        at = place if sending else order[r]
        return copy(out_send.at[a, order[r]], ref.at[:, part(at)], out_ssem.at[a, r], out_rsem.at[a, r], base + order[r])

    def start_hop(hop, b):
        for c in hop_copies(hop, b):
            c.start()

    def wait_hop(hop, b):
        for c in hop_copies(hop, b):
            c.wait_recv()

    def work(dz, b, c0, c1, causal, write_dq):
        n = (c1 - c0) * tok
        rows = slice(c0 * tok, c1 * tok)
        live = key_seg[rows, :] == stat[dz, b, 8:9, :]
        if causal:
            key_pos = lax.broadcasted_iota(jnp.int32, (n, tok), 0) + c0 * tok
            query_pos = lax.broadcasted_iota(jnp.int32, (n, tok), 1) + b * tok
            live = live & (key_pos <= query_pos)
        bias = jnp.where(live, 0.0, -1e30)

        def head(h, carry):
            here = pl.ds(pl.multiple_of(h * HEAD_DIM, HEAD_DIM), HEAD_DIM)
            qb, gb = visit[dz, b, 0, :, here], visit[dz, b, 1, :, here]
            kk, vv = keys[rows, here], values[rows, here]
            scores = dot(kk, qb, 1, 1) * (SCALE * LOG2E) - stat[dz, b, pl.ds(h + heads, 1), :]
            prob = jnp.exp2(scores + bias)
            prob_grad = dot(vv, gb, 1, 1)
            score_low = (prob * (prob_grad - stat[dz, b, pl.ds(h, 1), :])).astype(jnp.bfloat16)
            dv_acc[rows, here] += dot(prob.astype(jnp.bfloat16), gb, 1, 0)
            dk_acc[rows, here] += dot(score_low, qb, 1, 0)
            write_dq(here, dot(score_low, kk, 0, 0))
            return carry

        lax.fori_loop(0, heads, head, 0)

    for a in (0, 1, 2):
        for r in (2, 3, 1):
            in_copy(a, r, True).start()

    @pl.when(prev1)
    def _():
        start_hop(0, place)

    for a in (3, 4):
        for r in (2, 3, 1):
            in_copy(a, r, True).start()

    for r in range(1, GROUP):
        for a in (0, 1, 2):
            in_copy(a, r, False).wait_recv()

        @pl.when(prev1)
        def _(r=r):
            start_hop(0, order[r])

    for b in range(GROUP):
        seg = jnp.broadcast_to(stat[0, b, 8:9, :], (tok, tok))
        key_seg[b * tok : (b + 1) * tok, :] = seg.T
    for r in range(1, GROUP):
        for a in (3, 4):
            in_copy(a, r, False).wait_recv()

    for b in range(GROUP):

        def own(here, value, b=b):
            dq_acc[b, :, here] = value

        work(0, b, 0, b + 1, True, own)

    for r in range(GROUP):
        b = order[r]

        @pl.when(next1)
        def _(b=b):
            wait_hop(0, b)

            @pl.when(prev1 & (b < GROUP - 1))
            def _():
                start_hop(1, b)

            def visiting(here, value):
                dq_send[0, b, :, here] = value.astype(jnp.bfloat16)

            work(1, b, 0, GROUP, False, visiting)
            dq_copy(0, b).start()

    for b in range(GROUP - 1):

        @pl.when(next2)
        def _(b=b):
            wait_hop(1, b)

            def visiting(here, value):
                dq_send[1, b, :, here] = value.astype(jnp.bfloat16)

            work(2, b, b + 1, GROUP, False, visiting)
            dq_copy(1, b).start()

    def finish(a, acc, ref, r):
        if r == 0:
            ref[:, part(place)] = acc.astype(jnp.bfloat16)
        else:
            out_send[a, order[r]] = acc.astype(jnp.bfloat16)
            out_copy(a, r, True).start()

    for r in (2, 3, 1, 0):
        finish(1, dk_acc[rows_of(order[r]), :] * SCALE, dk_ref, r)
        finish(2, dv_acc[rows_of(order[r]), :], dv_ref, r)

    for r in (2, 3, 1, 0):
        b = order[r]

        @pl.when(prev1)
        def _(b=b):
            dq_copy(0, b).wait_recv()
            dq_acc[b] += dq_recv[0, b].astype(jnp.float32)

        @pl.when(prev2 & (b < GROUP - 1))
        def _(b=b):
            dq_copy(1, b).wait_recv()
            dq_acc[b] += dq_recv[1, b].astype(jnp.float32)

        finish(0, dq_acc[b] * SCALE, dq_ref, r)

    for r in range(1, GROUP):
        for a in range(5):
            in_copy(a, r, True).wait_send()
        for a in range(3):
            out_copy(a, r, True).wait_send()
            out_copy(a, r, False).wait_recv()

    for b in range(GROUP):

        @pl.when(prev1)
        def _(b=b):
            for c in hop_copies(0, b):
                c.wait_send()

        @pl.when(next1)
        def _(b=b):
            dq_copy(0, b).wait_send()

    for b in range(GROUP - 1):

        @pl.when(prev1 & next1)
        def _(b=b):
            for c in hop_copies(1, b):
                c.wait_send()

        @pl.when(next2)
        def _(b=b):
            dq_copy(1, b).wait_send()


def on_device(queries, key_rows, value_rows, attn_out, out_grad, log_norm, segments):
    tok, width = queries.shape
    cols = width // GROUP
    chain_len = lax.axis_size("ctx")
    bf16, f32 = jnp.bfloat16, jnp.float32
    dma = pltpu.SemaphoreType.DMA
    vmem = pl.BlockSpec(memory_space=pltpu.VMEM)
    return pl.pallas_call(
        functools.partial(kernel, chain_len),
        out_shape=[jax.ShapeDtypeStruct((tok, width), bf16)] * 3,
        in_specs=[vmem] * 7,
        out_specs=[vmem] * 3,
        scratch_shapes=[
            pltpu.VMEM((GROUP, 16, tok), f32),
            pltpu.VMEM((3, GROUP, 2, tok, cols), bf16),
            pltpu.VMEM((3, GROUP, 16, tok), f32),
            pltpu.VMEM((GROUP * tok, cols), bf16),
            pltpu.VMEM((GROUP * tok, cols), bf16),
            pltpu.VMEM((GROUP * tok, tok), f32),
            pltpu.VMEM((GROUP * tok, cols), f32),
            pltpu.VMEM((GROUP * tok, cols), f32),
            pltpu.VMEM((GROUP, tok, cols), f32),
            pltpu.VMEM((2, GROUP, tok, cols), bf16),
            pltpu.VMEM((2, GROUP, tok, cols), bf16),
            pltpu.VMEM((3, GROUP, tok, cols), bf16),
            dma((5, GROUP)), dma((5, GROUP)),
            dma((2, 2, GROUP)), dma((2, 2, GROUP)),
            dma((2, GROUP)), dma((2, GROUP)),
            dma((3, GROUP)), dma((3, GROUP)),
        ],
        compiler_params=pltpu.CompilerParams(
            collective_id=0, has_side_effects=True, vmem_limit_bytes=40 * 1024 * 1024
        ),
        name="attention_backward",
    )(queries, key_rows, value_rows, attn_out, out_grad, log_norm, segments.reshape(1, tok))


def solution(mesh):
    placed = (P(("dp", "ctx"), None),) * 6 + (P(("dp", "ctx")),)
    return jax.shard_map(
        on_device,
        mesh=mesh,
        in_specs=placed,
        out_specs=(P(("dp", "ctx"), None),) * 3,
        check_vma=False,
    )
```

time: 280 us -> 85.6 us (0.31)
  the two profiles are of different devices: /device:TPU:1 before, /device:TPU:0 now
where the time goes in v1:
time: 85.6 us; the launch traced here: 85.2 us
  Pallas kernels  76.2 us (89%)
  local copies, waits for them, and re-layouts  8.39 us (10%)
    pallas_call x1, Pallas kernels, on_device(): pl.pallas_call(functools.partial(kernel, chain_len), out_shape=[jax.Shape...  76.2 us
    unnamed x16, local copies, waits for them, and re-layouts  8.39 us

profile of v1, /device:TPU:0, one launch (start us, length us, event | category | flops | bytes accessed | tf_op | source)
XLA Modules:
  0.0 85.2 jit_solution(1794440556272605269)
XLA Ops:
  0.6 0.0 copy-start.5
  0.6 0.8 copy.10.ln_ref
  1.4 0.0 copy-done.5
  1.4 0.0 copy-start
  1.5 1.0 %copy-done = bf16[128,2048]{1,0:T(8,128)(2,1)S(1)} copy-done((bf16[128,2048]{1,0:T(8,128)(2,1)S(1)}, bf16[128,2048]{1,0:T(8,128)(2,1)}, u32[]{:S(2)}) %copy-start) | copy-done | bytes 524312
  2.5 0.0 copy-start.1
  2.5 1.0 %copy-done.1 = bf16[128,2048]{1,0:T(8,128)(2,1)S(1)} copy-done((bf16[128,2048]{1,0:T(8,128)(2,1)S(1)}, bf16[128,2048]{1,0:T(8,128)(2,1)}, u32[]{:S(2)}) %copy-start.1) | copy-done | bytes 524312
  3.5 0.0 copy-start.2
  3.5 1.0 %copy-done.2 = bf16[128,2048]{1,0:T(8,128)(2,1)S(1)} copy-done((bf16[128,2048]{1,0:T(8,128)(2,1)S(1)}, bf16[128,2048]{1,0:T(8,128)(2,1)}, u32[]{:S(2)}) %copy-start.2) | copy-done | bytes 524312
  4.6 0.0 copy-start.3
  4.6 1.0 %copy-done.3 = bf16[128,2048]{1,0:T(8,128)(2,1)S(1)} copy-done((bf16[128,2048]{1,0:T(8,128)(2,1)S(1)}, bf16[128,2048]{1,0:T(8,128)(2,1)}, u32[]{:S(2)}) %copy-start.3) | copy-done | bytes 524312
  5.6 0.0 copy-start.4
  5.6 1.0 %copy-done.4 = bf16[128,2048]{1,0:T(8,128)(2,1)S(1)} copy-done((bf16[128,2048]{1,0:T(8,128)(2,1)S(1)}, bf16[128,2048]{1,0:T(8,128)(2,1)}, u32[]{:S(2)}) %copy-start.4) | copy-done | bytes 524312
  6.7 76.2 %attention_backward.1 = (bf16[128,2048]{1,0:T(8,128)(2,1)S(1)}, bf16[128,2048]{1,0:T(8,128)(2,1)S(1)}, bf16[128,2048]{1,0:T(8,128)(2,1)S(1)}) custom-call(bf16[128,2048]{1,0:T(8,128)(2,1)S(1)} %copy-done, bf16[128,2048]{1,0:T(8,128)(2,1)S(1)} %copy-done.1, bf16[128,2048]{1,0:T(8,128)(2,1)S(1)} %copy-done.2, bf16[128,2048]{1,0:T(8,128)(2,1)S(1)} %copy-done.3, ...), custom_call_target="tpu_custom_call" | custom-call | tf_op jit(solution)/shard_map/attention_backward/pallas_call | solution.py:271
  82.8 0.8 copy.14
  83.6 0.8 copy.15
  84.4 0.8 copy.16
Async XLA Ops:
  0.6 0.8 copy-start.5
  1.4 1.0 %copy-start = (bf16[128,2048]{1,0:T(8,128)(2,1)S(1)}, bf16[128,2048]{1,0:T(8,128)(2,1)}, u32[]{:S(2)}) copy-start(bf16[128,2048]{1,0:T(8,128)(2,1)} %q_ref.1) | copy-start | bytes 1572868
  2.5 1.0 %copy-start.1 = (bf16[128,2048]{1,0:T(8,128)(2,1)S(1)}, bf16[128,2048]{1,0:T(8,128)(2,1)}, u32[]{:S(2)}) copy-start(bf16[128,2048]{1,0:T(8,128)(2,1)} %k_ref.1) | copy-start | bytes 1572868
  3.5 1.0 %copy-start.2 = (bf16[128,2048]{1,0:T(8,128)(2,1)S(1)}, bf16[128,2048]{1,0:T(8,128)(2,1)}, u32[]{:S(2)}) copy-start(bf16[128,2048]{1,0:T(8,128)(2,1)} %v_ref.1) | copy-start | bytes 1572868
  4.6 1.0 %copy-start.3 = (bf16[128,2048]{1,0:T(8,128)(2,1)S(1)}, bf16[128,2048]{1,0:T(8,128)(2,1)}, u32[]{:S(2)}) copy-start(bf16[128,2048]{1,0:T(8,128)(2,1)} %o_ref.1) | copy-start | bytes 1572868
  5.6 1.0 %copy-start.4 = (bf16[128,2048]{1,0:T(8,128)(2,1)S(1)}, bf16[128,2048]{1,0:T(8,128)(2,1)}, u32[]{:S(2)}) copy-start(bf16[128,2048]{1,0:T(8,128)(2,1)} %g_ref.1) | copy-start | bytes 1572868

commit v2 on v1

v2 whole, which is shorter than its diff:
```python
import functools

import jax
import jax.numpy as jnp
from jax import lax
from jax.experimental import pallas as pl
from jax.experimental.pallas import tpu as pltpu
from jax.sharding import PartitionSpec as P

HEAD_DIM = 128
SEQ_DEVS = 8
GROUP = 4
STAGES = 4
LOG2E = 1.4426950408889634
MESH = pl.DeviceIdType.MESH
SCALE = HEAD_DIM ** (-0.5)


def dot(a, b, a_dim, b_dim):
    return lax.dot_general(a, b, (((a_dim,), (b_dim,)), ((), ())), preferred_element_type=jnp.float32)


def kernel(
    chain_len,
    q_ref, k_ref, v_ref, o_ref, g_ref, ln_ref, seg_ref,
    dq_ref, dk_ref, dv_ref,
    o_all, g_all,
    stat_send, visit, stat, keys, values, key_seg, dk_acc, dv_acc, dq_acc,
    dq_send, dq_recv, out_send,
    own_sem, stat_ssem, stat_rsem, in_ssem, in_rsem, hop_ssem, hop_rsem, dq_ssem, dq_rsem, out_ssem, out_rsem,
):
    tok = q_ref.shape[0]
    cols = q_ref.shape[1] // GROUP
    heads = cols // HEAD_DIM
    stages, wide = visit.shape[1], visit.shape[5]
    stage_heads = wide // HEAD_DIM
    me = lax.axis_index("ctx")
    layer = me // GROUP
    place = me % GROUP
    layers = chain_len // GROUP
    base = layer * GROUP
    step = 1 - 2 * (place % 2)

    def nth(r):
        return (place + (r % 2) * step + 2 * (r // 2)) % GROUP

    prev1, prev2 = layer >= 1, layer >= 2
    next1, next2 = layer <= layers - 2, layer <= layers - 3

    def part(p, s):
        return pl.ds(pl.multiple_of(p * cols + s * wide, wide), wide)

    def rows_of(b):
        return pl.ds(pl.multiple_of(b * tok, tok), tok)

    def copy(src, dst, ssem, rsem, to):
        return pltpu.make_async_remote_copy(
            src_ref=src, dst_ref=dst, send_sem=ssem, recv_sem=rsem,
            device_id={"ctx": to}, device_id_type=MESH,
        )

    barrier = pltpu.get_barrier_semaphore()

    def greet(to):
        pl.semaphore_signal(barrier, inc=1, device_id={"ctx": to}, device_id_type=MESH)

    for r in range(1, GROUP):
        greet(base + nth(r))
    for there, to in ((prev1, me - GROUP), (prev2, me - 2 * GROUP), (next1, me + GROUP), (next2, me + 2 * GROUP)):
        pl.when(there)(functools.partial(greet, to))

    def in_ends(a, p, s, at):
        src = (q_ref, g_ref, k_ref, v_ref)[a].at[:, part(p, s)]
        dst = (visit.at[0, s, at, 0], visit.at[0, s, at, 1], keys.at[s, rows_of(at)], values.at[s, rows_of(at)])[a]
        return src, dst

    def own_copy(a, s):
        src, dst = in_ends(a, place, s, place)
        return pltpu.make_async_copy(src, dst, own_sem.at[a, s])

    def in_copy(a, r, s, sending):
        p = nth(r)
        src, dst = in_ends(a, p, s, place if sending else p)
        return copy(src, dst, in_ssem.at[a, r, s], in_rsem.at[a, r, s], base + p)

    def stat_copy(r, sending):
        p = nth(r)
        at = place if sending else p
        return copy(stat_send.at[p], stat.at[0, at], stat_ssem.at[0, r], stat_rsem.at[0, r], base + p)

    def stat_hop(hop, b):
        return copy(stat.at[hop, b], stat.at[hop + 1, b], stat_ssem.at[hop + 1, b], stat_rsem.at[hop + 1, b], me - GROUP)

    def hop_copy(hop, b, s):
        return copy(
            visit.at[hop, s, b], visit.at[hop + 1, s, b], hop_ssem.at[hop, b, s], hop_rsem.at[hop, b, s], me - GROUP
        )

    def dq_copy(d, b, s):
        return copy(
            dq_send.at[d, s, b], dq_recv.at[d, s, b], dq_ssem.at[d, b, s], dq_rsem.at[d, b, s], me + (d + 1) * GROUP
        )

    def out_copy(a, r, s, sending):
        ref = (dq_ref, dk_ref, dv_ref)[a]
        p = nth(r)
        at = place if sending else p
        return copy(
            out_send.at[a, s, p], ref.at[:, part(at, s)], out_ssem.at[a, r, s], out_rsem.at[a, r, s], base + p
        )

    o_copy = pltpu.make_async_copy(o_ref, o_all, own_sem.at[4, 0])
    g_copy = pltpu.make_async_copy(g_ref, g_all, own_sem.at[4, 1])
    o_copy.start()
    g_copy.start()
    for s in range(stages):
        for a in range(4):
            own_copy(a, s).start()
    partners = 3 + prev1.astype(jnp.int32) + prev2.astype(jnp.int32) + next1.astype(jnp.int32) + next2.astype(jnp.int32)
    pl.semaphore_wait(barrier, partners)

    def work(dz, b, c0, c1, s, causal, write_dq):
        n = (c1 - c0) * tok
        rows = slice(c0 * tok, c1 * tok)
        live = key_seg[rows, :] == stat[dz, b, 8:9, :]
        if causal:
            key_pos = lax.broadcasted_iota(jnp.int32, (n, tok), 0) + c0 * tok
            query_pos = lax.broadcasted_iota(jnp.int32, (n, tok), 1) + b * tok
            live = live & (key_pos <= query_pos)
        bias = jnp.where(live, 0.0, -1e30)
        for h in range(stage_heads):
            here = slice(h * HEAD_DIM, (h + 1) * HEAD_DIM)
            row = s * stage_heads + h
            qb, gb = visit[dz, s, b, 0, :, here], visit[dz, s, b, 1, :, here]
            kk, vv = keys[s, rows, here], values[s, rows, here]
            scores = dot(kk, qb, 1, 1) * (SCALE * LOG2E) - stat[dz, b, pl.ds(row + heads, 1), :]
            prob = jnp.exp2(scores + bias)
            prob_grad = dot(vv, gb, 1, 1)
            score_low = (prob * (prob_grad - stat[dz, b, pl.ds(row, 1), :])).astype(jnp.bfloat16)
            dv_add = dot(prob.astype(jnp.bfloat16), gb, 1, 0)
            dk_add = dot(score_low, qb, 1, 0)
            dv_acc[s, rows, here] += dv_add
            dk_acc[s, rows, here] += dk_add
            write_dq(here, dot(score_low, kk, 0, 0))

    def start_in(arrays, s):
        for r in (2, 3, 1):
            for a in arrays:
                in_copy(a, r, s, True).start()

    def finish(a, acc, ref, r, s):
        if r == 0:
            ref[:, part(place, s)] = acc.astype(jnp.bfloat16)
        else:
            out_send[a, s, nth(r)] = acc.astype(jnp.bfloat16)
            out_copy(a, r, s, True).start()

    def own_hop(s):
        for a in (0, 1):
            own_copy(a, s).wait()

        @pl.when(prev1)
        def _():
            hop_copy(0, place, s).start()

    def own_stage(s):
        for r in range(1, GROUP):
            for a in (0, 1):
                in_copy(a, r, s, False).wait_recv()

            @pl.when(prev1)
            def _(r=r):
                hop_copy(0, nth(r), s).start()

    def own_work(s):
        for a in (2, 3):
            own_copy(a, s).wait()
            for r in range(1, GROUP):
                in_copy(a, r, s, False).wait_recv()
        dk_acc[s] = jnp.zeros(dk_acc.shape[1:], jnp.float32)
        dv_acc[s] = jnp.zeros(dv_acc.shape[1:], jnp.float32)
        for b in range(GROUP):

            def own(here, value, b=b):
                dq_acc[s, b, :, here] = value

            work(0, b, 0, b + 1, s, True, own)

    def forward(s):
        for r in range(GROUP):
            b = nth(r)
            hop_copy(0, b, s).wait_recv()

            @pl.when(prev1 & (b < GROUP - 1))
            def _(b=b):
                hop_copy(1, b, s).start()

    def stat_arrived():
        for r in range(GROUP):
            b = nth(r)
            stat_hop(0, b).wait_recv()

            @pl.when(prev1 & (b < GROUP - 1))
            def _(b=b):
                stat_hop(1, b).start()

    def next_work(s):
        def one(r, carry):
            b = nth(r)

            def visiting(here, value):
                dq_send[0, s, b, :, here] = value.astype(jnp.bfloat16)

            work(1, b, 0, GROUP, s, False, visiting)
            dq_copy(0, b, s).start()
            return carry

        lax.fori_loop(0, GROUP, one, 0)

    def last_work(s):
        for b in range(GROUP - 1):

            @pl.when(s == 0)
            def _(b=b):
                stat_hop(1, b).wait_recv()

            hop_copy(1, b, s).wait_recv()

            def visiting(here, value, b=b):
                dq_send[1, s, b, :, here] = value.astype(jnp.bfloat16)

            work(2, b, b + 1, GROUP, s, False, visiting)
            dq_copy(1, b, s).start()

    def key_results(s):
        for r in (2, 3, 1, 0):
            finish(1, dk_acc[s, rows_of(nth(r)), :] * SCALE, dk_ref, r, s)
            finish(2, dv_acc[s, rows_of(nth(r)), :], dv_ref, r, s)

    def query_results(s):
        for r in (2, 3, 1, 0):
            b = nth(r)

            @pl.when(prev1)
            def _(b=b):
                dq_copy(0, b, s).wait_recv()
                dq_acc[s, b] += dq_recv[0, s, b].astype(jnp.float32)

            @pl.when(prev2 & (b < GROUP - 1))
            def _(b=b):
                dq_copy(1, b, s).wait_recv()
                dq_acc[s, b] += dq_recv[1, s, b].astype(jnp.float32)

            finish(0, dq_acc[s, b] * SCALE, dq_ref, r, s)

    start_in((0, 1), 0)
    own_hop(0)
    if stages > 1:
        own_hop(1)
    o_copy.wait()
    g_copy.wait()

    lane = lax.broadcasted_iota(jnp.int32, (tok, 128), 1)
    table = jnp.zeros((tok, 128), jnp.float32)
    for h in range(GROUP * heads):
        here = slice(h * HEAD_DIM, (h + 1) * HEAD_DIM)
        delta = jnp.sum(g_all[:, here].astype(jnp.float32) * o_all[:, here].astype(jnp.float32), axis=1, keepdims=True)
        table = jnp.where(lane == (h // heads) * 8 + h % heads, delta, table)
    table = table.T
    seg_rows = jnp.broadcast_to(seg_ref[...].astype(jnp.float32), (8, tok))
    for p in range(GROUP):
        stat_send[p, 0:heads, :] = table[8 * p : 8 * p + heads, :]
        stat_send[p, heads : 2 * heads, :] = ln_ref[p * heads : (p + 1) * heads, :] * LOG2E
        stat_send[p, 8:16, :] = seg_rows
    stat[0, place] = stat_send[place]

    for r in (2, 3, 1):
        stat_copy(r, True).start()
    own_stage(0)
    if stages > 1:
        start_in((0, 1), 1)
    start_in((2, 3), 0)
    for r in range(GROUP):
        if r:
            stat_copy(r, False).wait_recv()

        @pl.when(prev1)
        def _(r=r):
            stat_hop(0, nth(r)).start()

    for b in range(GROUP):
        seg = jnp.broadcast_to(stat[0, b, 8:9, :], (tok, tok))
        key_seg[b * tok : (b + 1) * tok, :] = seg.T

    def turn(i, carry):
        @pl.when(i + 1 < stages)
        def _():
            own_stage(i + 1)

        @pl.when(i + 2 < stages)
        def _():
            start_in((0, 1), i + 2)
            own_hop(i + 2)

        @pl.when((i < stages) & next1)
        def _():
            pl.when(i == 0)(stat_arrived)
            forward(i)

        @pl.when(i < stages)
        def _():
            own_work(i)

        @pl.when(i + 1 < stages)
        def _():
            start_in((2, 3), i + 1)

        @pl.when((i < stages) & next1)
        def _():
            next_work(i)

        @pl.when((i >= 1) & (i <= stages))
        def _():
            pl.when(next2)(functools.partial(last_work, i - 1))
            key_results(i - 1)

        @pl.when(i >= 2)
        def _():
            query_results(i - 2)

        return carry

    lax.fori_loop(0, stages + 2, turn, 0)

    for r in range(1, GROUP):
        stat_copy(r, True).wait_send()
    for b in range(GROUP):
        pl.when(prev1)(stat_hop(0, b).wait_send)
        if b < GROUP - 1:
            pl.when(prev1 & next1)(stat_hop(1, b).wait_send)

    def drain(s, carry):
        for r in range(1, GROUP):
            for a in range(4):
                in_copy(a, r, s, True).wait_send()
            for a in range(3):
                out_copy(a, r, s, True).wait_send()
                out_copy(a, r, s, False).wait_recv()
        for b in range(GROUP):
            pl.when(prev1)(hop_copy(0, b, s).wait_send)
            pl.when(next1)(dq_copy(0, b, s).wait_send)
            if b < GROUP - 1:
                pl.when(prev1 & next1)(hop_copy(1, b, s).wait_send)
                pl.when(next2)(dq_copy(1, b, s).wait_send)
        return carry

    lax.fori_loop(0, stages, drain, 0)


def on_device(queries, key_rows, value_rows, attn_out, out_grad, log_norm, segments):
    tok, width = queries.shape
    cols = width // GROUP
    stages = STAGES
    wide = cols // stages
    chain_len = lax.axis_size("ctx")
    bf16, f32 = jnp.bfloat16, jnp.float32
    dma = pltpu.SemaphoreType.DMA
    vmem = pl.BlockSpec(memory_space=pltpu.VMEM)
    far = pl.BlockSpec(memory_space=pl.ANY)
    return pl.pallas_call(
        functools.partial(kernel, chain_len),
        out_shape=[jax.ShapeDtypeStruct((tok, width), bf16)] * 3,
        in_specs=[far] * 5 + [vmem] * 2,
        out_specs=[vmem] * 3,
        scratch_shapes=[
            pltpu.VMEM((tok, width), bf16),
            pltpu.VMEM((tok, width), bf16),
            pltpu.VMEM((GROUP, 16, tok), f32),
            pltpu.VMEM((3, stages, GROUP, 2, tok, wide), bf16),
            pltpu.VMEM((3, GROUP, 16, tok), f32),
            pltpu.VMEM((stages, GROUP * tok, wide), bf16),
            pltpu.VMEM((stages, GROUP * tok, wide), bf16),
            pltpu.VMEM((GROUP * tok, tok), f32),
            pltpu.VMEM((stages, GROUP * tok, wide), f32),
            pltpu.VMEM((stages, GROUP * tok, wide), f32),
            pltpu.VMEM((stages, GROUP, tok, wide), f32),
            pltpu.VMEM((2, stages, GROUP, tok, wide), bf16),
            pltpu.VMEM((2, stages, GROUP, tok, wide), bf16),
            pltpu.VMEM((3, stages, GROUP, tok, wide), bf16),
            dma((5, max(stages, 2))),
            dma((3, GROUP)), dma((3, GROUP)),
            dma((4, GROUP, stages)), dma((4, GROUP, stages)),
            dma((2, GROUP, stages)), dma((2, GROUP, stages)),
            dma((2, GROUP, stages)), dma((2, GROUP, stages)),
            dma((3, GROUP, stages)), dma((3, GROUP, stages)),
        ],
        compiler_params=pltpu.CompilerParams(
            collective_id=0, has_side_effects=True, vmem_limit_bytes=40 * 1024 * 1024
        ),
        name="attention_backward",
    )(queries, key_rows, value_rows, attn_out, out_grad, log_norm.T, segments.reshape(1, tok))


def solution(mesh):
    placed = (P(("dp", "ctx"), None),) * 6 + (P(("dp", "ctx")),)
    return jax.shard_map(
        on_device,
        mesh=mesh,
        in_specs=placed,
        out_specs=(P(("dp", "ctx"), None),) * 3,
        check_vma=False,
    )
```

time: 85.6 us -> 68.4 us (0.80)
  Pallas kernels: 76.2 us -> 58.4 us
    pallas_call x1, Pallas kernels: 76.2 us -> 58.4 us  [on_device(): pl.pallas_call(functools.partial(kernel, chain_len), out_shape=[jax.Shape...]
    unnamed x16 -> x17, local copies, waits for them, and re-layouts: 8.39 us -> 8.93 us
where the time goes in v2:
time: 68.4 us; the launch traced here: 68 us
  Pallas kernels  58.4 us (85%)
  local copies, waits for them, and re-layouts  8.93 us (13%)
    pallas_call x1, Pallas kernels, on_device(): pl.pallas_call(functools.partial(kernel, chain_len), out_shape=[jax.Shape...  58.4 us
    unnamed x17, local copies, waits for them, and re-layouts  8.93 us

profile of v2, /device:TPU:0, one launch (start us, length us, event | category | flops | bytes accessed | tf_op | source)
XLA Modules:
  0.0 68.0 jit_solution(2862279995151601395)
XLA Ops:
  0.6 0.0 copy-start.6
  0.6 0.6 copy-done.6
  1.3 0.0 copy-start
  1.3 1.0 %copy-done = bf16[128,2048]{1,0:T(8,128)(2,1)S(1)} copy-done((bf16[128,2048]{1,0:T(8,128)(2,1)S(1)}, bf16[128,2048]{1,0:T(8,128)(2,1)}, u32[]{:S(2)}) %copy-start) | copy-done | bytes 524312
  2.3 0.0 copy-start.1
  2.3 1.0 %copy-done.1 = bf16[128,2048]{1,0:T(8,128)(2,1)S(1)} copy-done((bf16[128,2048]{1,0:T(8,128)(2,1)S(1)}, bf16[128,2048]{1,0:T(8,128)(2,1)}, u32[]{:S(2)}) %copy-start.1) | copy-done | bytes 524312
  3.4 0.0 copy-start.2
  3.4 1.0 %copy-done.2 = bf16[128,2048]{1,0:T(8,128)(2,1)S(1)} copy-done((bf16[128,2048]{1,0:T(8,128)(2,1)S(1)}, bf16[128,2048]{1,0:T(8,128)(2,1)}, u32[]{:S(2)}) %copy-start.2) | copy-done | bytes 524312
  4.4 0.0 copy-start.3
  4.4 1.0 %copy-done.3 = bf16[128,2048]{1,0:T(8,128)(2,1)S(1)} copy-done((bf16[128,2048]{1,0:T(8,128)(2,1)S(1)}, bf16[128,2048]{1,0:T(8,128)(2,1)}, u32[]{:S(2)}) %copy-start.3) | copy-done | bytes 524312
  5.5 0.0 copy-start.4
  5.5 1.0 %copy-done.4 = bf16[128,2048]{1,0:T(8,128)(2,1)S(1)} copy-done((bf16[128,2048]{1,0:T(8,128)(2,1)S(1)}, bf16[128,2048]{1,0:T(8,128)(2,1)}, u32[]{:S(2)}) %copy-start.4) | copy-done | bytes 524312
  6.5 0.0 copy-start.5
  6.5 0.7 %copy-done.5 = f32[128,16]{0,1:T(8,128)S(1)} copy-done((f32[128,16]{0,1:T(8,128)S(1)}, f32[128,16]{0,1:T(8,128)}, u32[]{:S(2)}) %copy-start.5) | copy-done | bytes 8216
  7.2 58.4 %attention_backward.1 = (bf16[128,2048]{1,0:T(8,128)(2,1)S(1)}, bf16[128,2048]{1,0:T(8,128)(2,1)S(1)}, bf16[128,2048]{1,0:T(8,128)(2,1)S(1)}) custom-call(bf16[128,2048]{1,0:T(8,128)(2,1)S(1)} %copy-done, bf16[128,2048]{1,0:T(8,128)(2,1)S(1)} %copy-done.1, bf16[128,2048]{1,0:T(8,128)(2,1)S(1)} %copy-done.2, bf16[128,2048]{1,0:T(8,128)(2,1)S(1)} %copy-done.3, ...), custom_call_target="tpu_custom_call" | custom-call | tf_op jit(solution)/shard_map/attention_backward/pallas_call | solution.py:370
  65.6 0.8 %copy.13 = bf16[128,2048]{1,0:T(8,128)(2,1)} copy(bf16[128,2048]{1,0:T(8,128)(2,1)S(1)} %get-tuple-element.6) | data formatting | bytes 1048576
  66.4 0.8 %copy.14 = bf16[128,2048]{1,0:T(8,128)(2,1)} copy(bf16[128,2048]{1,0:T(8,128)(2,1)S(1)} %get-tuple-element.7) | data formatting | bytes 1048576
  67.2 0.8 %copy.15 = bf16[128,2048]{1,0:T(8,128)(2,1)} copy(bf16[128,2048]{1,0:T(8,128)(2,1)S(1)} %get-tuple-element.8) | data formatting | bytes 1048576
Async XLA Ops:
  0.6 0.7 copy-start.6
  1.3 1.0 %copy-start = (bf16[128,2048]{1,0:T(8,128)(2,1)S(1)}, bf16[128,2048]{1,0:T(8,128)(2,1)}, u32[]{:S(2)}) copy-start(bf16[128,2048]{1,0:T(8,128)(2,1)} %q_ref.1) | copy-start | bytes 1572868
  2.3 1.0 %copy-start.1 = (bf16[128,2048]{1,0:T(8,128)(2,1)S(1)}, bf16[128,2048]{1,0:T(8,128)(2,1)}, u32[]{:S(2)}) copy-start(bf16[128,2048]{1,0:T(8,128)(2,1)} %k_ref.1) | copy-start | bytes 1572868
  3.4 1.0 %copy-start.2 = (bf16[128,2048]{1,0:T(8,128)(2,1)S(1)}, bf16[128,2048]{1,0:T(8,128)(2,1)}, u32[]{:S(2)}) copy-start(bf16[128,2048]{1,0:T(8,128)(2,1)} %v_ref.1) | copy-start | bytes 1572868
  4.4 1.0 %copy-start.3 = (bf16[128,2048]{1,0:T(8,128)(2,1)S(1)}, bf16[128,2048]{1,0:T(8,128)(2,1)}, u32[]{:S(2)}) copy-start(bf16[128,2048]{1,0:T(8,128)(2,1)} %o_ref.1) | copy-start | bytes 1572868
  5.5 1.0 %copy-start.4 = (bf16[128,2048]{1,0:T(8,128)(2,1)S(1)}, bf16[128,2048]{1,0:T(8,128)(2,1)}, u32[]{:S(2)}) copy-start(bf16[128,2048]{1,0:T(8,128)(2,1)} %g_ref.1) | copy-start | bytes 1572868
  6.5 0.7 %copy-start.5 = (f32[128,16]{0,1:T(8,128)S(1)}, f32[128,16]{0,1:T(8,128)}, u32[]{:S(2)}) copy-start(f32[128,16]{0,1:T(8,128)} %param.12) | copy-start | bytes 24580

commit v3 on v2

--- a/solution.py
+++ b/solution.py
@@ -22,9 +22,9 @@
 
 def kernel(
     chain_len,
-    q_ref, k_ref, v_ref, o_ref, g_ref, ln_ref, seg_ref,
+    q_ref, k_ref, v_ref, o_ref, g_ref, ln_far, seg_far,
     dq_ref, dk_ref, dv_ref,
-    o_all, g_all,
+    o_all, g_all, ln_ref, seg_ref,
     stat_send, visit, stat, keys, values, key_seg, dk_acc, dv_acc, dq_acc,
     dq_send, dq_recv, out_send,
     own_sem, stat_ssem, stat_rsem, in_ssem, in_rsem, hop_ssem, hop_rsem, dq_ssem, dq_rsem, out_ssem, out_rsem,
@@ -111,10 +111,12 @@
 
     o_copy = pltpu.make_async_copy(o_ref, o_all, own_sem.at[4, 0])
     g_copy = pltpu.make_async_copy(g_ref, g_all, own_sem.at[4, 1])
-    o_copy.start()
-    g_copy.start()
-    for s in range(stages):
-        for a in range(4):
+    ln_copy = pltpu.make_async_copy(ln_far, ln_ref, own_sem.at[4, 2])
+    seg_copy = pltpu.make_async_copy(seg_far, seg_ref, own_sem.at[4, 3])
+    for c in (o_copy, g_copy, ln_copy, seg_copy):
+        c.start()
+    for a in range(4):
+        for s in range(stages):
             own_copy(a, s).start()
     partners = 3 + prev1.astype(jnp.int32) + prev2.astype(jnp.int32) + next1.astype(jnp.int32) + next2.astype(jnp.int32)
     pl.semaphore_wait(barrier, partners)
@@ -254,11 +256,12 @@
             finish(0, dq_acc[s, b] * SCALE, dq_ref, r, s)
 
     start_in((0, 1), 0)
-    own_hop(0)
-    if stages > 1:
-        own_hop(1)
+    for s in range(stages):
+        own_hop(s)
     o_copy.wait()
     g_copy.wait()
+    ln_copy.wait()
+    seg_copy.wait()
 
     lane = lax.broadcasted_iota(jnp.int32, (tok, 128), 1)
     table = jnp.zeros((tok, 128), jnp.float32)
@@ -300,7 +303,6 @@
         @pl.when(i + 2 < stages)
         def _():
             start_in((0, 1), i + 2)
-            own_hop(i + 2)
 
         @pl.when((i < stages) & next1)
         def _():
@@ -366,15 +368,17 @@
     bf16, f32 = jnp.bfloat16, jnp.float32
     dma = pltpu.SemaphoreType.DMA
     vmem = pl.BlockSpec(memory_space=pltpu.VMEM)
-    far = pl.BlockSpec(memory_space=pl.ANY)
+    far = pl.BlockSpec(memory_space=pltpu.HBM)
     return pl.pallas_call(
         functools.partial(kernel, chain_len),
         out_shape=[jax.ShapeDtypeStruct((tok, width), bf16)] * 3,
-        in_specs=[far] * 5 + [vmem] * 2,
+        in_specs=[far] * 7,
         out_specs=[vmem] * 3,
         scratch_shapes=[
             pltpu.VMEM((tok, width), bf16),
             pltpu.VMEM((tok, width), bf16),
+            pltpu.VMEM(log_norm.shape[::-1], f32),
+            pltpu.VMEM((1, tok), jnp.int32),
             pltpu.VMEM((GROUP, 16, tok), f32),
             pltpu.VMEM((3, stages, GROUP, 2, tok, wide), bf16),
             pltpu.VMEM((3, GROUP, 16, tok), f32),
@@ -387,7 +391,7 @@
             pltpu.VMEM((2, stages, GROUP, tok, wide), bf16),
             pltpu.VMEM((2, stages, GROUP, tok, wide), bf16),
             pltpu.VMEM((3, stages, GROUP, tok, wide), bf16),
-            dma((5, max(stages, 2))),
+            dma((5, max(stages, 4))),
             dma((3, GROUP)), dma((3, GROUP)),
             dma((4, GROUP, stages)), dma((4, GROUP, stages)),
             dma((2, GROUP, stages)), dma((2, GROUP, stages)),
@@ -395,7 +399,7 @@
             dma((3, GROUP, stages)), dma((3, GROUP, stages)),
         ],
         compiler_params=pltpu.CompilerParams(
-            collective_id=0, has_side_effects=True, vmem_limit_bytes=40 * 1024 * 1024
+            collective_id=0, has_side_effects=True, vmem_limit_bytes=62 * 1024 * 1024
         ),
         name="attention_backward",
     )(queries, key_rows, value_rows, attn_out, out_grad, log_norm.T, segments.reshape(1, tok))

time: 68.4 us -> 64.4 us (0.942)
  local copies, waits for them, and re-layouts: 8.93 us -> 3.97 us
  Pallas kernels: 58.4 us -> 59.6 us
    unnamed x17 -> x7, local copies, waits for them, and re-layouts: 8.93 us -> 3.97 us
    pallas_call x1, Pallas kernels: 58.4 us -> 59.6 us  [on_device(): pl.pallas_call(functools.partial(kernel, chain_len), out_shape=[jax.Shape...]
where the time goes in v3:
time: 64.4 us; the launch traced here: 64.2 us
  Pallas kernels  59.6 us (93%)
  local copies, waits for them, and re-layouts  3.97 us (6%)
  between operations  0.65 us (1%)
    pallas_call x1, Pallas kernels, on_device(): pl.pallas_call(functools.partial(kernel, chain_len), out_shape=[jax.Shape...  59.6 us
    unnamed x7, local copies, waits for them, and re-layouts  3.97 us

profile of v3, /device:TPU:0, one launch (start us, length us, event | category | flops | bytes accessed | tf_op | source)
XLA Modules:
  0.0 64.2 jit_solution(4293184683104749805)
XLA Ops:
  0.6 59.6 %attention_backward.1 = (bf16[128,2048]{1,0:T(8,128)(2,1)}, bf16[128,2048]{1,0:T(8,128)(2,1)}, bf16[128,2048]{1,0:T(8,128)(2,1)}) custom-call(bf16[128,2048]{1,0:T(8,128)(2,1)} %q_ref.1, bf16[128,2048]{1,0:T(8,128)(2,1)} %k_ref.1, bf16[128,2048]{1,0:T(8,128)(2,1)} %v_ref.1, bf16[128,2048]{1,0:T(8,128)(2,1)} %o_ref.1, bf16[128,2048]{1,0:T(8,128)(2,1)} %g_ref.1, ...), custom_call_target="tpu_custom_call" | custom-call | tf_op jit(solution)/shard_map/attention_backward/pallas_call | solution.py:372
  60.2 0.0 copy-start.1
  60.2 1.9 %copy.13 = bf16[128,2048]{1,0:T(8,128)(2,1)} copy(bf16[128,2048]{1,0:T(8,128)(2,1)} %get-tuple-element.6) | data formatting | bytes 1048576
  62.1 0.0 copy-done.1
  62.1 0.0 copy-start
  62.1 0.8 %copy.14 = bf16[128,2048]{1,0:T(8,128)(2,1)} copy(bf16[128,2048]{1,0:T(8,128)(2,1)S(1)} %copy-done.1) | data formatting | bytes 1048576
  62.9 0.4 copy-done
  63.4 0.8 %copy.15 = bf16[128,2048]{1,0:T(8,128)(2,1)} copy(bf16[128,2048]{1,0:T(8,128)(2,1)S(1)} %copy-done) | data formatting | bytes 1048576
Async XLA Ops:
  60.2 2.0 %copy-start.1 = (bf16[128,2048]{1,0:T(8,128)(2,1)S(1)}, bf16[128,2048]{1,0:T(8,128)(2,1)}, u32[]{:S(2)}) copy-start(bf16[128,2048]{1,0:T(8,128)(2,1)} %get-tuple-element.7) | copy-start | bytes 1572868
  62.1 1.2 %copy-start = (bf16[128,2048]{1,0:T(8,128)(2,1)S(1)}, bf16[128,2048]{1,0:T(8,128)(2,1)}, u32[]{:S(2)}) copy-start(bf16[128,2048]{1,0:T(8,128)(2,1)} %get-tuple-element.8) | copy-start | bytes 1572868

commit v4 on v3

--- a/solution.py
+++ b/solution.py
@@ -150,11 +150,15 @@
             for a in arrays:
                 in_copy(a, r, s, True).start()
 
+    def out_own(a, s):
+        ref = (dq_ref, dk_ref, dv_ref)[a]
+        return pltpu.make_async_copy(out_send.at[a, s, place], ref.at[:, part(place, s)], out_ssem.at[a, 0, s])
+
     def finish(a, acc, ref, r, s):
+        out_send[a, s, nth(r)] = acc.astype(jnp.bfloat16)
         if r == 0:
-            ref[:, part(place, s)] = acc.astype(jnp.bfloat16)
+            out_own(a, s).start()
         else:
-            out_send[a, s, nth(r)] = acc.astype(jnp.bfloat16)
             out_copy(a, r, s, True).start()
 
     def own_hop(s):
@@ -342,6 +346,8 @@
             pl.when(prev1 & next1)(stat_hop(1, b).wait_send)
 
     def drain(s, carry):
+        for a in range(3):
+            out_own(a, s).wait()
         for r in range(1, GROUP):
             for a in range(4):
                 in_copy(a, r, s, True).wait_send()
@@ -367,13 +373,12 @@
     chain_len = lax.axis_size("ctx")
     bf16, f32 = jnp.bfloat16, jnp.float32
     dma = pltpu.SemaphoreType.DMA
-    vmem = pl.BlockSpec(memory_space=pltpu.VMEM)
     far = pl.BlockSpec(memory_space=pltpu.HBM)
     return pl.pallas_call(
         functools.partial(kernel, chain_len),
         out_shape=[jax.ShapeDtypeStruct((tok, width), bf16)] * 3,
         in_specs=[far] * 7,
-        out_specs=[vmem] * 3,
+        out_specs=[far] * 3,
         scratch_shapes=[
             pltpu.VMEM((tok, width), bf16),
             pltpu.VMEM((tok, width), bf16),

time: 64.4 us -> 63.3 us (0.983)
  Pallas kernels: 59.6 us -> 58.5 us
    pallas_call x1, Pallas kernels: 59.6 us -> 58.5 us  [on_device(): pl.pallas_call(functools.partial(kernel, chain_len), out_shape=[jax.Shape...]
where the time goes in v4:
time: 63.3 us; the launch traced here: 63.1 us
  Pallas kernels  58.5 us (92%)
  local copies, waits for them, and re-layouts  3.97 us (6%)
  between operations  0.65 us (1%)
    pallas_call x1, Pallas kernels, on_device(): pl.pallas_call(functools.partial(kernel, chain_len), out_shape=[jax.Shape...  58.5 us
    unnamed x7, local copies, waits for them, and re-layouts  3.97 us

profile of v4, /device:TPU:0, one launch (start us, length us, event | category | flops | bytes accessed | tf_op | source)
XLA Modules:
  0.0 63.1 jit_solution(3195943898109969332)
XLA Ops:
  0.6 58.5 %attention_backward.1 = (bf16[128,2048]{1,0:T(8,128)(2,1)}, bf16[128,2048]{1,0:T(8,128)(2,1)}, bf16[128,2048]{1,0:T(8,128)(2,1)}) custom-call(bf16[128,2048]{1,0:T(8,128)(2,1)} %q_ref.1, bf16[128,2048]{1,0:T(8,128)(2,1)} %k_ref.1, bf16[128,2048]{1,0:T(8,128)(2,1)} %v_ref.1, bf16[128,2048]{1,0:T(8,128)(2,1)} %o_ref.1, bf16[128,2048]{1,0:T(8,128)(2,1)} %g_ref.1, ...), custom_call_target="tpu_custom_call" | custom-call | tf_op jit(solution)/shard_map/attention_backward/pallas_call | solution.py:377
  59.1 0.0 copy-start.1
  59.1 1.9 %copy.13 = bf16[128,2048]{1,0:T(8,128)(2,1)} copy(bf16[128,2048]{1,0:T(8,128)(2,1)} %get-tuple-element.6) | data formatting | bytes 1048576
  61.1 0.0 copy-done.1
  61.1 0.0 copy-start
  61.1 0.8 %copy.14 = bf16[128,2048]{1,0:T(8,128)(2,1)} copy(bf16[128,2048]{1,0:T(8,128)(2,1)S(1)} %copy-done.1) | data formatting | bytes 1048576
  61.9 0.4 copy-done
  62.3 0.8 %copy.15 = bf16[128,2048]{1,0:T(8,128)(2,1)} copy(bf16[128,2048]{1,0:T(8,128)(2,1)S(1)} %copy-done) | data formatting | bytes 1048576
Async XLA Ops:
  59.1 2.0 %copy-start.1 = (bf16[128,2048]{1,0:T(8,128)(2,1)S(1)}, bf16[128,2048]{1,0:T(8,128)(2,1)}, u32[]{:S(2)}) copy-start(bf16[128,2048]{1,0:T(8,128)(2,1)} %get-tuple-element.7) | copy-start | bytes 1572868
  61.1 1.2 %copy-start = (bf16[128,2048]{1,0:T(8,128)(2,1)S(1)}, bf16[128,2048]{1,0:T(8,128)(2,1)}, u32[]{:S(2)}) copy-start(bf16[128,2048]{1,0:T(8,128)(2,1)} %get-tuple-element.8) | copy-start | bytes 1572868
